TPU v7x, 256 devices: a whole 4x4x8 slice. The times are simulated.
256 devices in a mesh: row: 8 (over x, y_hi), col: 32 (over z, y_lo, core).
Axes of the slice: x: 4, y: 4 (y_hi: 2, y_lo: 2; y = y_hi * 2 + y_lo), z: 8, core: 2. Of those that a mesh axis runs over, the one named last changes fastest.
Arguments:
- pair: bfloat16 [256, 256, 128], P('row', 'col'), may hold values from -6 to 6
- pair_mask: int32 [256, 256], P('row', 'col'), may hold values 0 or 1
- ln_in_gain: float32 [128], replicated, may hold values from 0.1 to 1.9
- w_ab: bfloat16 [128, 512], replicated, may hold values from -0.5 to 0.5
- w_gate: bfloat16 [128, 128], replicated, may hold values from -0.5 to 0.5
- ln_out_gain: float32 [128], replicated, may hold values from 0.1 to 1.9
- w_out: bfloat16 [128, 128], replicated, may hold values from -0.5 to 0.5
- cotangent: bfloat16 [256, 256, 128], P('row', 'col'), may hold values from -6 to 6
Outputs:
- update: bfloat16 [256, 256, 128], P('row', 'col')
- grad_pair: bfloat16 [256, 256, 128], P('row', 'col')
- grad_w_ab: float32 [128, 512], replicated
- grad_w_gate: float32 [128, 128], replicated
- grad_w_out: float32 [128, 128], replicated
All inputs are finite; a program needn't handle non-finite values. No bound on the sum of `pair_mask` on one device may be relied on, other than what follows from the above.
Results may differ from a plain program's by a relative error of at most 0.025.
Values may be sent and summed in bfloat16 or wider, within the bound.
No kernel may reach another device: no remote copies, remote signals or barrier semaphores. Data moves between devices by JAX's collectives and lax.ppermute only.
A program may use at most 64 MiB of HBM per device.

v0:
```python
import jax
import jax.numpy as jnp
from jax import lax
from jax.sharding import PartitionSpec as P


def spread(array, axis, root):
    mine = lax.axis_index(axis) == root
    return lax.psum(jnp.where(mine, array, jnp.zeros_like(array)), axis)


def layer_norm(values):
    center = values - jnp.mean(values, axis=-1, keepdims=True)
    inverse = lax.rsqrt(jnp.mean(center * center, axis=-1, keepdims=True) + 1e-05)
    return (center * inverse, inverse)


def norm_back(grad_h, normed, inverse):
    first = jnp.mean(grad_h, axis=-1, keepdims=True)
    second = jnp.mean(grad_h * normed, axis=-1, keepdims=True)
    return inverse * (grad_h - first - normed * second)


def outer_sum(left, right):
    return lax.dot_general(
        left, right, (((0,), (0,)), ((), ())), preferred_element_type=jnp.float32
    )


def right_transposed(left, right):
    return lax.dot_general(
        left, right, (((1,), (1,)), ((), ())), preferred_element_type=jnp.float32
    )


def on_device(pair, pair_mask, ln_in_gain, w_ab, w_gate, ln_out_gain, w_out, cotangent):
    rows_i, cols_j, width = pair.shape
    hidden = w_out.shape[0]
    col_count = lax.axis_size("col")
    ratio = rows_i // cols_j
    col_index = lax.axis_index("col")
    full_res = cols_j * col_count
    flat_pairs = rows_i * cols_j
    h_in, inv_in = layer_norm(pair.astype(jnp.float32))
    normed_in = (h_in * ln_in_gain).astype(jnp.bfloat16)
    flat_in = normed_in.reshape(flat_pairs, width)
    proj = jnp.dot(flat_in, w_ab, preferred_element_type=jnp.float32).reshape(
        rows_i, cols_j, 4 * hidden
    )
    a_gate = proj[..., 0:hidden]
    a_value = proj[..., hidden : 2 * hidden]
    b_gate = proj[..., 2 * hidden : 3 * hidden]
    b_value = proj[..., 3 * hidden : 4 * hidden]
    mask_f = pair_mask.astype(jnp.float32)[..., None]
    sig_a = jax.nn.sigmoid(a_gate)
    sig_b = jax.nn.sigmoid(b_gate)
    a_tile = (mask_f * sig_a * a_value).astype(jnp.bfloat16)
    b_tile = (mask_f * sig_b * b_value).astype(jnp.bfloat16)
    gate = jax.nn.sigmoid(jnp.dot(flat_in, w_gate, preferred_element_type=jnp.float32)).reshape(
        rows_i, cols_j, width
    )
    b_stripe = lax.all_gather(b_tile, "col", axis=1, tiled=True)
    b_local = lax.dynamic_slice_in_dim(b_stripe, col_index % ratio * cols_j, cols_j, 0)
    b_rows = spread(b_local, "row", col_index // ratio)
    a_stripe = lax.all_gather(a_tile, "col", axis=1, tiled=True)
    mixed = jnp.einsum("ikc,jkc->ijc", a_stripe, b_rows, preferred_element_type=jnp.float32)
    h_out, inv_out = layer_norm(mixed)
    normed_out = (h_out * ln_out_gain).astype(jnp.bfloat16)
    flat_out = normed_out.reshape(flat_pairs, hidden)
    y_val = jnp.dot(flat_out, w_out, preferred_element_type=jnp.float32).reshape(
        rows_i, cols_j, width
    )
    update = (gate * y_val).astype(jnp.bfloat16)
    cot_f32 = cotangent.astype(jnp.float32)
    d_y = (cot_f32 * gate).astype(jnp.bfloat16).reshape(flat_pairs, width)
    d_gate = (cot_f32 * y_val * gate * (1.0 - gate)).astype(jnp.bfloat16).reshape(flat_pairs, width)
    local_w_out = outer_sum(flat_out, d_y)
    d_normed = right_transposed(d_y, w_out).reshape(rows_i, cols_j, hidden)
    d_mixed = norm_back(d_normed * ln_out_gain, h_out, inv_out).astype(jnp.bfloat16)
    d_a = jnp.transpose(
        lax.psum_scatter(
            jnp.einsum("ijc,jkc->kic", d_mixed, b_rows, preferred_element_type=jnp.float32).astype(
                jnp.bfloat16
            ),
            "col",
            scatter_dimension=0,
            tiled=True,
        ).astype(jnp.float32),
        (1, 0, 2),
    )
    b_partial = jnp.einsum("ijc,ikc->jkc", d_mixed, a_stripe, preferred_element_type=jnp.float32)
    outgoing_grads = b_partial.reshape(cols_j, col_count, cols_j, hidden)
    received_grads = lax.all_to_all(
        outgoing_grads.astype(jnp.bfloat16), "col", split_axis=1, concat_axis=0, tiled=True
    ).astype(outgoing_grads.dtype)
    d_b = lax.psum_scatter(
        received_grads.reshape(full_res, cols_j, hidden).astype(jnp.bfloat16),
        "row",
        scatter_dimension=0,
        tiled=True,
    ).astype(jnp.float32)
    d_a_value = d_a * mask_f * sig_a
    d_a_gate = d_a * mask_f * a_value * sig_a * (1.0 - sig_a)
    d_b_value = d_b * mask_f * sig_b
    d_b_gate = d_b * mask_f * b_value * sig_b * (1.0 - sig_b)
    d_proj = jnp.concatenate([d_a_gate, d_a_value, d_b_gate, d_b_value], axis=-1).astype(
        jnp.bfloat16
    )
    d_proj = d_proj.reshape(flat_pairs, 4 * hidden)
    local_w_ab = outer_sum(flat_in, d_proj)
    local_w_gate = outer_sum(flat_in, d_gate)
    d_in = right_transposed(d_proj, w_ab) + right_transposed(d_gate, w_gate)
    d_in = d_in.reshape(rows_i, cols_j, width)
    grad_pair = norm_back(d_in * ln_in_gain, h_in, inv_in).astype(jnp.bfloat16)
    sum_ab, sum_gate, sum_out = lax.psum((local_w_ab, local_w_gate, local_w_out), ("row", "col"))
    return (update, grad_pair, sum_ab / full_res, sum_gate / full_res, sum_out / full_res)


def solution(mesh):
    placed = (
        P("row", "col", None),
        P("row", "col"),
        P(),
        P(),
        P(),
        P(),
        P(),
        P("row", "col", None),
    )
    return jax.shard_map(
        on_device,
        mesh=mesh,
        in_specs=placed,
        out_specs=(P("row", "col", None), P("row", "col", None), P(), P(), P()),
        check_vma=False,
    )
```

profile of v0, /device:TPU:1, one launch (start us, length us, event | category | flops | bytes accessed | tf_op | source)
XLA Modules:
  0.0 732.0 jit_solution(13273793080607794500)
XLA Ops:
  7.2 0.0 copy-start
  7.2 0.0 copy-start.12
  7.2 0.0 all-gather.3.cloned.1.call-start
  7.3 1.0 convert_reduce_fusion
  8.2 0.1 copy.84
  8.3 0.1 copy.85
  8.4 1.0 fusion.29
  9.4 0.1 copy.86
  9.5 0.1 copy.87
  9.6 0.7 convert_element_type.64
  10.3 0.1 copy.88
  10.4 1.1 fusion.40
  11.5 0.8 multiply_convert_fusion.5
  12.2 0.0 all-gather.3.cloned.1.call-update
  12.3 0.0 all-gather.5.cloned.1.call-start
  12.3 0.7 all-gather.5.cloned.1.call-update
  13.0 0.0 all-reduce.4.cloned.1.call-start
  13.1 69.5 %all-gather.3.cloned.1.call-done = bf16[32,256,128]{2,1,0:T(8,128)(2,1)} async-done(((bf16[32,8,128]{2,1,0:T(8,128)(2,1)}), bf16[32,256,128]{2,1,0:T(8,128)(2,1)}) %all-gather.3.cloned.1.call-update) | async-done | bytes 2097168 | tf_op jit(solution)/shard_map/all_gather | solution.py:62
  82.6 1.9 dynamic-slice_select_fusion
  84.5 0.0 all-reduce.4.cloned.1.call-update
  84.5 0.0 reduce-scatter.5.cloned.1.call-start
  84.6 1.1 fusion.4
  85.7 0.6 copy-done.4
  86.3 0.2 fusion.51
  86.5 0.3 copy.92
  86.8 62.2 %all-gather.5.cloned.1.call-done = bf16[32,256,128]{2,1,0:T(8,128)(2,1)} async-done(((bf16[32,8,128]{2,1,0:T(8,128)(2,1)}), bf16[32,256,128]{2,1,0:T(8,128)(2,1)}) %all-gather.5.cloned.1.call-update) | async-done | bytes 2097168 | tf_op jit(solution)/shard_map/all_gather | solution.py:65
  149.0 15.3 %copy.90 = bf16[32,256,128]{0,1,2:T(8,128)(2,1)} copy(bf16[32,256,128]{2,1,0:T(8,128)(2,1)} %all-gather.5.cloned.1.call-done) | data formatting | bytes 4194304 | tf_op jit(solution)/shard_map/all_gather | solution.py:65
  164.3 70.4 %all-reduce.4.cloned.1.call-done = bf16[8,256,128]{2,1,0:T(8,128)(2,1)} async-done(((bf16[8,256,128]{2,1,0:T(8,128)(2,1)}), bf16[8,256,128]{2,1,0:T(8,128)(2,1)}) %all-reduce.4.cloned.1.call-update) | async-done | bytes 524304 | tf_op jit(solution)/shard_map/psum | solution.py:9
  234.7 1.4 copy.89
  236.2 4.7 fusion.63
  240.9 0.2 multiply_reduce_fusion.1
  241.1 0.2 multiply_reduce_fusion.2
  241.3 0.9 multiply_convert_fusion
  242.3 2.3 fusion
  244.5 0.5 copy.96
  245.0 0.1 copy.97
  245.1 29.7 %all_to_all.18 = bf16[8,32,8,128]{3,2,0,1:T(8,128)(2,1)} all-to-all(bf16[8,32,8,128]{3,2,0,1:T(8,128)(2,1)S(1)} %copy.97), channel_id=1, replica_groups=mesh['row'=8,'col'=32] {'col'}, dimensions={1} | all-to-all | bytes 1048576 | tf_op jit(solution)/shard_map/all_to_all | solution.py:93
  274.8 0.0 reduce-scatter.5.cloned.1.call-update
  274.9 0.0 reduce-scatter.7.cloned.1.call-start
  274.9 0.8 convert_bitcast_fusion
  275.7 4.0 copy.101
  279.7 4.0 copy.106
  283.7 0.0 reduce-scatter.7.cloned.1.call-update
  283.7 0.0 all-reduce.6.cloned.1.call-start
  283.8 0.2 copy.91
  284.0 0.8 fusion.33
  284.8 1.0 convolution_bitcast_fusion.3
  285.8 0.8 convolution_bitcast_fusion.2
  286.6 0.2 fusion.48
  286.8 57.0 %reduce-scatter.5.cloned.1.call-done = bf16[32,8,128]{2,1,0:T(8,128)(2,1)} async-done(((bf16[256,8,128]{2,1,0:T(8,128)(2,1)}), bf16[32,8,128]{2,1,0:T(8,128)(2,1)}) %reduce-scatter.5.cloned.1.call-update) | async-done | bytes 65552 | tf_op jit(solution)/shard_map/reduce_scatter | solution.py:96
  343.8 118.2 %reduce-scatter.7.cloned.1.call-done = bf16[8,4096]{1,0:T(8,128)(2,1)} async-done(((bf16[256,4096]{1,0:T(8,128)(2,1)}), bf16[8,4096]{1,0:T(8,128)(2,1)}) %reduce-scatter.7.cloned.1.call-update) | async-done | bytes 65552
  461.9 1.0 fusion.46
  463.0 1.0 convolution_bitcast_fusion.1
  464.0 0.3 fusion.25
  464.3 0.1 copy.98
  464.4 0.1 copy.99
  464.5 0.1 multiply_reduce_fusion.3
  464.6 0.1 div.68
  464.7 0.0 all-reduce.6.cloned.1.call-update
  464.7 0.8 fusion.28
  465.5 255.0 %all-reduce.6.cloned.1.call-done = (f32[128,512]{1,0:T(8,128)}, f32[128,128]{1,0:T(8,128)}, f32[128,128]{1,0:T(8,128)}) async-done(((f32[128,512]{1,0:T(8,128)}, f32[128,128]{1,0:T(8,128)}, f32[128,128]{1,0:T(8,128)}), (f32[128,512]{1,0:T(8,128)}, f32[128,128]{1,0:T(8,128)}, f32[128,128]{1,0:T(8,128)})) %all-reduce.6.cloned.1.call-update) | async-done | bytes 393232 | tf_op jit(solution)/shard_map/psum | solution.py:115
  720.5 1.7 broadcast_multiply_fusion
  722.2 1.5 broadcast_multiply_fusion.1
  723.7 1.5 broadcast_multiply_fusion.2
  (38 shorter events, 0.1 us)
Async XLA Ops:
  7.2 3.2 copy-start
  7.2 79.1 %copy-start.12 = (bf16[128,128]{1,0:T(8,128)(2,1)S(1)}, bf16[128,128]{1,0:T(8,128)(2,1)}, u32[]{:S(2)}) copy-start(bf16[128,128]{1,0:T(8,128)(2,1)} %param.14) | copy-start | bytes 98308
  7.2 79.1 %copy-start.6 = (bf16[32,8,128]{2,1,0:T(8,128)(2,1)S(1)}, bf16[32,8,128]{2,1,0:T(8,128)(2,1)}, u32[]{:S(2)}) copy-start(bf16[32,8,128]{2,1,0:T(8,128)(2,1)} %param.15) | copy-start | bytes 196612
  7.2 75.4 %all-gather.3.cloned.1.call-start = ((), (), s32[]{:S(2)}) async-start(), calls=%async_computation.3 | async-start | bytes 2162688 | tf_op jit(solution)/shard_map/all_gather | solution.py:62
  9.6 75.0 %copy-start.8 = (f32[32,8]{1,0:T(8,128)}, f32[32,8]{1,0:T(8,128)S(1)}, u32[]{:S(2)}) copy-start(f32[32,8]{1,0:T(8,128)S(1)} %copy.87) | copy-start | bytes 3076
  10.4 74.2 %copy-start.10 = (f32[32,8]{1,0:T(8,128)}, f32[32,8]{1,0:T(8,128)S(1)}, u32[]{:S(2)}) copy-start(f32[32,8]{1,0:T(8,128)S(1)} %copy.88) | copy-start | bytes 3076
  12.3 136.7 %all-gather.5.cloned.1.call-start = ((), (), s32[]{:S(2)}) async-start(), calls=%async_computation.5 | async-start | bytes 2162688 | tf_op jit(solution)/shard_map/all_gather | solution.py:65
  13.0 221.7 %all-reduce.4.cloned.1.call-start = ((), (), s32[]{:S(2)}) async-start(), calls=%async_computation.4 | async-start | bytes 1048576 | tf_op jit(solution)/shard_map/psum | solution.py:9
  84.5 259.3 %reduce-scatter.5.cloned.1.call-start = ((), (), s32[]{:S(2)}) async-start(), calls=%async_computation.6 | async-start | bytes 589824 | tf_op jit(solution)/shard_map/reduce_scatter | solution.py:96
  85.7 0.6 copy-start.4
  236.2 4.9 copy-start.16
  236.2 6.1 copy-start.1
  274.9 187.1 %reduce-scatter.7.cloned.1.call-start = ((), (), s32[]{:S(2)}) async-start(), calls=%async_computation.7 | async-start | bytes 2162688
  279.7 4.1 copy-start.3
  279.7 4.3 copy-start.5
  279.7 4.3 copy-start.7
  279.7 4.3 copy-start.13
  279.7 5.2 copy-start.2
  279.7 5.1 copy-start.9
  279.7 5.1 copy-start.15
  279.7 6.9 copy-start.14
  279.7 182.2 %copy-start.11 = (f32[32,8]{1,0:T(8,128)S(1)}, f32[32,8]{1,0:T(8,128)}, u32[]{:S(2)}) copy-start(f32[32,8]{1,0:T(8,128)} %copy-done.10) | copy-start | bytes 3076
  283.7 436.8 %all-reduce.6.cloned.1.call-start = ((), (), s32[]{:S(2)}) async-start(), calls=%async_computation.8 | async-start | bytes 786432 | tf_op jit(solution)/shard_map/psum | solution.py:115
Sparse Core Ops, SparseCore 0:
  12.4 70.1 all-gather.2
  84.9 64.0 all-gather.4
  151.6 83.0 all-reduce.3
  275.0 68.7 reduce-scatter.4
  346.1 115.7 reduce-scatter.6
  469.2 251.2 all-reduce.5
where the time goes:
time: 733 us; the launch traced here: 732 us
  waiting for transfers between devices  633 us (86%)
  blocking collectives  29.7 us (4%)
  local copies, waits for them, and re-layouts  27 us (4%)
  between operations  14.4 us (2%)
  matrix products  14.2 us (2%)
  other arithmetic  13.3 us (2%)
    psum x1, waiting for transfers between devices, on_device(): lax.psum((local_w_ab, local_w_gate, local_w_out), ('row', 'col'))  255 us
    unnamed x7, waiting for transfers between devices  119 us
    psum x1, waiting for transfers between devices, spread(): return lax.psum(jnp.where(mine, array, jnp.zeros_like(array)), axis)  70.4 us
    all_gather x1, waiting for transfers between devices, on_device(): b_stripe = lax.all_gather(b_tile, 'col', axis=1, tiled=True)  69.5 us
    all_gather x1, waiting for transfers between devices, on_device(): a_stripe = lax.all_gather(a_tile, 'col', axis=1, tiled=True)  62.2 us
    reduce_scatter x1, waiting for transfers between devices, on_device(): lax.psum_scatter(received_grads.reshape(full_res, cols_j, hidden).astype(...  57 us
    all_to_all x1, blocking collectives, on_device(): lax.all_to_all(outgoing_grads.astype(jnp.bfloat16), 'col', split_axis=1,...  29.7 us
    all_gather x1, local copies, waits for them, and re-layouts, on_device(): a_stripe = lax.all_gather(a_tile, 'col', axis=1, tiled=True)  15.3 us
  transfers between devices with their start and end apart: 6, of which 6 were waited for; matrix products, arithmetic and copies ran while one was open for 4% of the time, Pallas kernels for 0%

commit v1 on v0

v1 whole, which is shorter than its diff:
```python
import jax
import jax.numpy as jnp
from jax import lax
from jax.experimental import pallas as pl
from jax.experimental.pallas import tpu as pltpu
from jax.sharding import PartitionSpec as P

F32 = jnp.float32
BF16 = jnp.bfloat16

ROWS, COLS, WIDTH = 32, 8, 128
NROW, NCOL = 8, 32
PAIRS = ROWS * COLS
GROUP = WIDTH // NCOL
RES = 256


def dot(left, right, left_dim, right_dim):
    return lax.dot_general(
        left, right, (((left_dim,), (right_dim,)), ((), ())), preferred_element_type=F32
    )


def lane_block(shape):
    return lax.broadcasted_iota(jnp.int32, shape, 1) // ROWS


def load_pairs(block, scratch):
    scratch[...] = block[...].astype(F32).reshape(PAIRS, WIDTH)
    return jnp.concatenate(
        [scratch[pl.ds(k, ROWS, stride=COLS), :] for k in range(COLS)], axis=0
    )


def store_pairs(values, scratch, block):
    for k in range(COLS):
        scratch[pl.ds(k, ROWS, stride=COLS), :] = values[k * ROWS : (k + 1) * ROWS]
    block[...] = scratch[...].reshape(ROWS, COLS, WIDTH).astype(block.dtype)


def regroup(scratch, blocks):
    return jnp.concatenate(
        [
            scratch[pl.ds(blk * WIDTH + c4, NCOL, stride=GROUP), :]
            for blk in range(blocks)
            for c4 in range(GROUP)
        ],
        axis=0,
    )


def ungroup(values, scratch, blocks):
    for blk in range(blocks):
        for c4 in range(GROUP):
            start = blk * WIDTH + c4 * NCOL
            scratch[pl.ds(blk * WIDTH + c4, NCOL, stride=GROUP), :] = values[start : start + NCOL]


def to_message(values, k):
    tile, place = k // GROUP, k % GROUP
    block = lane_block((NCOL, WIDTH))
    result = None
    for c4 in range(GROUP):
        part = values[c4 * NCOL : (c4 + 1) * NCOL, tile * WIDTH : (tile + 1) * WIDTH]
        shift = (c4 - place) * ROWS % WIDTH
        if shift:
            part = pltpu.roll(part, shift, 1)
        result = part if result is None else jnp.where(block == c4, part, result)
    return result


def from_message(pieces):
    block = lane_block((NCOL, WIDTH))
    bands = []
    for c4 in range(GROUP):
        tiles = []
        for tile in range(COLS // GROUP):
            result = None
            for place in range(GROUP):
                part = pieces[tile * GROUP + place]
                shift = (place - c4) * ROWS % WIDTH
                if shift:
                    part = pltpu.roll(part, shift, 1)
                result = part if result is None else jnp.where(block == place, part, result)
            tiles.append(result)
        bands.append(jnp.concatenate(tiles, axis=1))
    return jnp.concatenate(bands, axis=0)


def mask_rows(mask):
    flags = mask[...].astype(F32).astype(BF16)
    eye = (
        lax.broadcasted_iota(jnp.int32, (COLS, COLS), 0)
        == lax.broadcasted_iota(jnp.int32, (COLS, COLS), 1)
    ).astype(F32).astype(BF16)
    turned = dot(eye, flags, 1, 1).astype(BF16)
    spread = (
        lax.broadcasted_iota(jnp.int32, (ROWS, WIDTH), 1) % ROWS
        == lax.broadcasted_iota(jnp.int32, (ROWS, WIDTH), 0)
    ).astype(F32).astype(BF16)
    return dot(turned, spread, 1, 0)


def column_of(gain):
    row = lax.broadcasted_iota(jnp.int32, (WIDTH, WIDTH), 0)
    lane = lax.broadcasted_iota(jnp.int32, (WIDTH, WIDTH), 1)
    here = lane == (row % NCOL) * GROUP + row // NCOL
    return jnp.sum(jnp.where(here, gain, 0.0), axis=1, keepdims=True)


def layer_norm(values, axis):
    center = values - jnp.mean(values, axis=axis, keepdims=True)
    inverse = lax.rsqrt(jnp.mean(center * center, axis=axis, keepdims=True) + 1e-05)
    return center * inverse, inverse


def norm_back(grad_h, normed, inverse, axis):
    first = jnp.mean(grad_h, axis=axis, keepdims=True)
    second = jnp.mean(grad_h * normed, axis=axis, keepdims=True)
    return inverse * (grad_h - first - normed * second)


def halves(message):
    wide = message.astype(F32).reshape(NCOL, 2 * COLS, WIDTH)
    return wide[:, :COLS].reshape(PAIRS, WIDTH), wide[:, COLS:].reshape(PAIRS, WIDTH)


def project_kernel(pair, mask, gain, w_ab, normed_out, send, rows, weights, message):
    values = load_pairs(pair, rows)
    h_in, _ = layer_norm(values, 1)
    normed = (h_in * gain[...]).astype(BF16)
    normed_out[...] = normed
    weights[...] = w_ab[...].astype(F32).T
    proj = dot(regroup(weights, 4).astype(BF16), normed, 1, 1)
    a_val = jax.nn.sigmoid(proj[0:128]) * proj[128:256]
    b_val = jax.nn.sigmoid(proj[256:384]) * proj[384:512]
    flags = mask_rows(mask)
    for k in range(COLS):
        flag = flags[k : k + 1]
        message[pl.ds(k, NCOL, stride=2 * COLS), :] = to_message(a_val, k) * flag
        message[pl.ds(COLS + k, NCOL, stride=2 * COLS), :] = to_message(b_val, k) * flag
    send[...] = message[...].astype(BF16)


def mix_kernel(recv, b_all, send):
    a_val = halves(recv[...])[0].astype(BF16)
    block = lane_block((ROWS, WIDTH))
    for r in range(NROW):
        full = dot(b_all[r * RES : (r + 1) * RES], a_val, 0, 0)
        own = full[0:ROWS]
        for c4 in range(1, GROUP):
            own = jnp.where(block == c4, full[c4 * ROWS : (c4 + 1) * ROWS], own)
        send[r * ROWS : (r + 1) * ROWS] = own


def middle_kernel(
    recv, normed_in, cotangent, w_gate, gain, w_out,
    update, send, d_gate_out, grad_gate, grad_out, rows, weights,
):
    mixed = from_message([recv[pl.ds(k, NCOL, stride=COLS), :] for k in range(COLS)])
    h_out, inv_out = layer_norm(mixed, 0)
    scale = column_of(gain[...])
    normed = (h_out * scale).astype(BF16)
    weights[...] = w_out[...].astype(F32)
    w_own = regroup(weights, 1).astype(BF16)
    y_val = dot(normed, w_own, 0, 0)
    flat_in = normed_in[...]
    gate = jax.nn.sigmoid(dot(flat_in, w_gate[...], 1, 0))
    store_pairs(gate * y_val, rows, update)
    cot = load_pairs(cotangent, rows)
    d_y = (cot * gate).astype(BF16)
    d_gate = (cot * y_val * gate * (1.0 - gate)).astype(BF16)
    d_gate_out[...] = d_gate
    ungroup(dot(normed, d_y, 1, 0), weights, 1)
    grad_out[...] = weights[...]
    grad_gate[...] = dot(flat_in, d_gate, 0, 0)
    grad_h = dot(w_own, d_y, 1, 1) * scale
    d_mixed = norm_back(grad_h, h_out, inv_out, 0)
    for k in range(COLS):
        rows[pl.ds(k, NCOL, stride=COLS), :] = to_message(d_mixed, k)
    send[...] = rows[...].astype(BF16)


def grad_kernel(recv, b_all, d_mixed, d_a, d_b):
    a_val = halves(recv[...])[0].astype(BF16)
    own = (
        lax.broadcasted_iota(jnp.int32, (WIDTH, WIDTH), 0) // ROWS
        == lane_block((WIDTH, WIDTH))
    )
    total = None
    for r in range(NROW):
        part = d_mixed[r * ROWS : (r + 1) * ROWS].astype(F32)
        spread = jnp.where(own, jnp.concatenate([part] * GROUP, axis=0), 0.0).astype(BF16)
        term = dot(b_all[r * RES : (r + 1) * RES], spread, 1, 0)
        total = term if total is None else total + term
        d_b[r * RES : (r + 1) * RES] = dot(a_val, spread, 1, 1).astype(BF16)
    d_a[...] = total


def join_kernel(d_a, d_b, send):
    total = d_b[0:RES].astype(F32)
    for r in range(1, NROW):
        total = total + d_b[r * RES : (r + 1) * RES].astype(F32)
    both = jnp.concatenate(
        [d_a[...].reshape(NCOL, COLS, WIDTH), total.reshape(NCOL, COLS, WIDTH)], axis=1
    )
    send[...] = both.reshape(2 * PAIRS, WIDTH).astype(BF16)


def last_kernel(
    recv, pair, mask, gain, w_ab, w_gate, normed_in, d_gate,
    grad_pair, grad_ab, rows, weights, message,
):
    values = load_pairs(pair, rows)
    h_in, inv_in = layer_norm(values, 1)
    flat_in = normed_in[...]
    weights[...] = w_ab[...].astype(F32).T
    w_own = regroup(weights, 4).astype(BF16)
    proj = dot(w_own, flat_in, 1, 1)
    flags = mask_rows(mask)
    message[...] = recv[...].astype(F32)
    grads = []
    for half in range(2):
        pieces = [
            message[pl.ds(half * COLS + k, NCOL, stride=2 * COLS), :] * flags[k : k + 1]
            for k in range(COLS)
        ]
        d_val = from_message(pieces)
        sig = jax.nn.sigmoid(proj[half * 256 : half * 256 + 128])
        value = proj[half * 256 + 128 : half * 256 + 256]
        d_value = d_val * sig
        grads += [d_value * value * (1.0 - sig), d_value]
    d_proj = jnp.concatenate(grads, axis=0).astype(BF16)
    d_in = dot(d_proj, w_own, 0, 0) + dot(d_gate[...], w_gate[...], 1, 1)
    store_pairs(norm_back(d_in * gain[...], h_in, inv_in, 1), rows, grad_pair)
    ungroup(dot(d_proj, flat_in, 1, 0), weights, 4)
    grad_ab[...] = weights[...]


def call(kernel, outs, scratch, *args):
    return pl.pallas_call(
        kernel,
        out_shape=[jax.ShapeDtypeStruct(shape, dtype) for shape, dtype in outs],
        scratch_shapes=[pltpu.VMEM(shape, F32) for shape in scratch],
        compiler_params=pltpu.CompilerParams(vmem_limit_bytes=32 * 1024 * 1024),
    )(*args)


def exchange(values, axis):
    return lax.all_to_all(values, axis, 0, 0, tiled=True)


def on_device(pair, pair_mask, ln_in_gain, w_ab, w_gate, ln_out_gain, w_out, cotangent):
    gain_in = ln_in_gain.reshape(1, WIDTH)
    gain_out = ln_out_gain.reshape(1, WIDTH)
    flat = (PAIRS, WIDTH)
    twice = (2 * PAIRS, WIDTH)
    copies = (NROW * RES, WIDTH)
    blocks = (ROWS, COLS, WIDTH)
    normed_in, send_ab = call(
        project_kernel,
        [(flat, BF16), (twice, BF16)],
        [flat, (4 * WIDTH, WIDTH), twice],
        pair, pair_mask, gain_in, w_ab,
    )
    recv_ab = exchange(send_ab, "col")
    b_own = recv_ab.reshape(NCOL, 2 * COLS, WIDTH)[:, COLS:].reshape(flat)
    b_all = exchange(jnp.broadcast_to(b_own[None], (NROW,) + flat).reshape(copies), "row")
    (send_mixed,) = call(mix_kernel, [(flat, F32)], [], recv_ab, b_all)
    recv_mixed = exchange(send_mixed, "col")
    update, send_d, d_gate, grad_gate, grad_out = call(
        middle_kernel,
        [(blocks, BF16), (flat, BF16), (flat, BF16), ((WIDTH, WIDTH), F32), ((WIDTH, WIDTH), F32)],
        [flat, (WIDTH, WIDTH)],
        recv_mixed, normed_in, cotangent, w_gate, gain_out, w_out,
    )
    d_mixed = exchange(send_d, "col")
    d_a, d_b = call(grad_kernel, [(flat, F32), (copies, BF16)], [], recv_ab, b_all, d_mixed)
    d_b = exchange(d_b, "row")
    (send_grads,) = call(join_kernel, [(twice, BF16)], [], d_a, d_b)
    recv_grads = exchange(send_grads, "col")
    grad_pair, grad_ab = call(
        last_kernel,
        [(blocks, BF16), ((4 * WIDTH, WIDTH), F32)],
        [flat, (4 * WIDTH, WIDTH), twice],
        recv_grads, pair, pair_mask, gain_in, w_ab, w_gate, normed_in, d_gate,
    )
    both = ("row", "col")
    local = jnp.concatenate([grad_ab, grad_gate, grad_out], axis=0).reshape(RES, 1, 3 * WIDTH)
    own = jnp.sum(exchange(local, both), axis=0, keepdims=True)
    total = exchange(jnp.broadcast_to(own, local.shape), both).reshape(6 * WIDTH, WIDTH) / RES
    return (
        update,
        grad_pair,
        total[: 4 * WIDTH].T,
        total[4 * WIDTH : 5 * WIDTH],
        total[5 * WIDTH :],
    )


def solution(mesh):
    placed = (
        P("row", "col", None),
        P("row", "col"),
        P(),
        P(),
        P(),
        P(),
        P(),
        P("row", "col", None),
    )
    return jax.shard_map(
        on_device,
        mesh=mesh,
        in_specs=placed,
        out_specs=(P("row", "col", None), P("row", "col", None), P(), P(), P()),
        check_vma=False,
    )
```

time: 733 us -> 148 us (0.20)
  waiting for transfers between devices: 633 us -> 0 us
  blocking collectives: 29.7 us -> 136 us
  local copies, waits for them, and re-layouts: 27 us -> 5.63 us
  matrix products: 14.2 us -> 0 us
  between operations: 14.4 us -> 0.73 us
  other arithmetic: 13.3 us -> 0.67 us
    psum x2 -> x0, waiting for transfers between devices: 325 us -> none  [the longest x1 255 us: on_device(): lax.psum((local_w_ab, local_w_gate, local_w_out), ('row', 'col'))]
    all_gather x2 -> x0, waiting for transfers between devices: 132 us -> none  [the longest x1 69.5 us: on_device(): b_stripe = lax.all_gather(b_tile, 'col', axis=1, tiled=True)]
    unnamed x7 -> x0, waiting for transfers between devices: 119 us -> none
    all_to_all x1 -> x8, blocking collectives: 29.7 us -> 136 us  [exchange(): return lax.all_to_all(values, axis, 0, 0, tiled=True)]
    reduce_scatter x1 -> x0, waiting for transfers between devices: 57 us -> none  [on_device(): lax.psum_scatter(received_grads.reshape(full_res, cols_j, hidden).astype(...]
    all_gather x1 -> x0, local copies, waits for them, and re-layouts: 15.3 us -> none  [on_device(): a_stripe = lax.all_gather(a_tile, 'col', axis=1, tiled=True)]
    dot_general x12 -> x0, matrix products: 14.2 us -> none  [the longest x1 4.72 us: on_device(): jnp.einsum('ikc,jkc->ijc', a_stripe, b_rows, preferred_element_type=jnp.f...]
  transfers between devices with their start and end apart: 6 -> 0, of which waited for: 6 -> 0; matrix products, arithmetic and copies ran while one was open for 4% -> 0% of each run, Pallas kernels for 0% -> 0%
where the time goes in v1:
time: 148 us
  blocking collectives  136 us (92%)
  local copies, waits for them, and re-layouts  5.63 us (4%)
  Pallas kernels  4.44 us (3%)
    all_to_all x8, blocking collectives, exchange(): return lax.all_to_all(values, axis, 0, 0, tiled=True)  136 us
    unnamed x20, local copies, waits for them, and re-layouts  4.67 us
    pallas_call x6, Pallas kernels, call(): pl.pallas_call(kernel, out_shape=[jax.ShapeDtypeStruct(shape, dtype) for...  4.44 us

profile of v1, /device:TPU:1, one launch (start us, length us, event | category | flops | bytes accessed | tf_op | source)
XLA Modules:
  0.0 147.9 jit_solution(6325506360068805692)
XLA Ops:
  0.6 0.8 copy.16.mask
  1.4 0.0 copy-start.7
  1.4 0.7 copy-done.7
  2.0 0.0 copy-start
  2.1 0.9 copy-done
  3.0 0.0 copy-start.2
  3.0 0.8 copy-done.2
  3.8 0.8 shard_map.119
  4.6 20.2 %all_to_all.73 = bf16[32,16,128]{2,1,0:T(8,128)(2,1)S(1)} all-to-all(bf16[32,16,128]{2,1,0:T(8,128)(2,1)S(1)} %bitcast.30), channel_id=1, replica_groups=mesh['row'=8,'col'=32] {'col'}, dimensions={0} | all-to-all | bytes 262144 | tf_op jit(solution)/shard_map/all_to_all | solution.py:250
  24.8 0.1 broadcast_in_dim.14
  24.8 15.9 %all_to_all.74 = bf16[8,256,128]{2,1,0:T(8,128)(2,1)S(1)} all-to-all(bf16[8,256,128]{2,1,0:T(8,128)(2,1)S(1)} %broadcast_in_dim.14), channel_id=1, replica_groups=mesh['row'=8,'col'=32] {'row'}, dimensions={0} | all-to-all | bytes 1048576 | tf_op jit(solution)/shard_map/all_to_all | solution.py:250
  40.7 0.3 shard_map.120
  41.1 0.0 copy-start.4
  41.1 0.0 copy-start.5
  41.1 0.0 copy-start.6
  41.1 14.7 %all_to_all.75 = f32[32,8,128]{2,1,0:T(8,128)S(1)} all-to-all(f32[32,8,128]{2,1,0:T(8,128)S(1)} %bitcast.28), channel_id=1, replica_groups=mesh['row'=8,'col'=32] {'col'}, dimensions={0} | all-to-all | bytes 262144 | tf_op jit(solution)/shard_map/all_to_all | solution.py:250
  55.8 0.0 copy-start.8
  55.8 0.0 copy-done.4
  55.8 0.0 copy-done.5
  55.8 0.0 copy-done.6
  55.8 0.6 copy-done.8
  56.4 1.3 shard_map.121
  57.8 11.5 %all_to_all.76 = bf16[32,8,128]{2,1,0:T(8,128)(2,1)S(1)} all-to-all(bf16[32,8,128]{2,1,0:T(8,128)(2,1)S(1)} %bitcast.31), channel_id=1, replica_groups=mesh['row'=8,'col'=32] {'col'}, dimensions={0} | all-to-all | bytes 131072 | tf_op jit(solution)/shard_map/all_to_all | solution.py:250
  69.3 0.4 shard_map.122
  69.7 12.6 %all_to_all.77 = bf16[8,256,128]{2,1,0:T(8,128)(2,1)S(1)} all-to-all(bf16[8,256,128]{2,1,0:T(8,128)(2,1)S(1)} %bitcast.26), channel_id=1, replica_groups=mesh['row'=8,'col'=32] {'row'}, dimensions={0} | all-to-all | bytes 1048576 | tf_op jit(solution)/shard_map/all_to_all | solution.py:250
  82.3 0.1 shard_map.123
  82.4 0.0 copy-start.1
  82.4 0.0 copy-start.3
  82.4 14.5 %all_to_all.78 = bf16[32,16,128]{2,1,0:T(8,128)(2,1)S(1)} all-to-all(bf16[32,16,128]{2,1,0:T(8,128)(2,1)S(1)} %bitcast.27), channel_id=1, replica_groups=mesh['row'=8,'col'=32] {'col'}, dimensions={0} | all-to-all | bytes 262144 | tf_op jit(solution)/shard_map/all_to_all | solution.py:250
  96.9 0.0 copy-done.1
  96.9 0.0 copy-done.3
  96.9 1.5 %shard_map.124 = (bf16[32,8,128]{2,1,0:T(8,128)(2,1)}, f32[512,128]{1,0:T(8,128)S(1)}) custom-call(bf16[512,128]{1,0:T(8,128)(2,1)S(1)} %bitcast.25, bf16[32,8,128]{2,1,0:T(8,128)(2,1)S(1)} %copy-done.3, s32[32,8]{1,0:T(8,128)S(1)} %copy.16.mask, f32[1,128]{1,0:T(1,128)S(1)} %bitcast.33, bf16[128,512]{1,0:T(8,128)(2,1)S(1)} %copy-done.1, ...), custom_call_target="tpu_custom_call" | custom-call | tf_op jit(solution)/shard_map/pallas_call | solution.py:241
  98.5 23.7 %all_to_all.79 = f32[256,1,384]{2,1,0:T(1,128)S(1)} all-to-all(f32[256,1,384]{2,1,0:T(1,128)S(1)} %bitcast.37), channel_id=1, replica_groups=mesh['row'=8,'col'=32] {'row','col'}, dimensions={0} | all-to-all | bytes 786432 | tf_op jit(solution)/shard_map/all_to_all | solution.py:250
  122.2 0.3 reduce_sum.9
  122.5 0.2 broadcast_in_dim.15
  122.7 23.4 %all_to_all.80 = f32[256,1,384]{2,1,0:T(1,128)S(1)} all-to-all(f32[256,1,384]{2,1,0:T(1,128)S(1)} %broadcast_in_dim.15), channel_id=1, replica_groups=mesh['row'=8,'col'=32] {'row','col'}, dimensions={0} | all-to-all | bytes 786432 | tf_op jit(solution)/shard_map/all_to_all | solution.py:250
  146.0 0.3 broadcast_multiply_fusion
  146.4 0.7 fusion
  147.1 0.8 copy.19
  (3 shorter events, 0.1 us)
Async XLA Ops:
  1.4 0.7 copy-start.7
  2.0 0.9 copy-start
  3.0 0.8 copy-start.2
  41.1 14.7 %copy-start.4 = (bf16[128,128]{1,0:T(8,128)(2,1)S(1)}, bf16[128,128]{1,0:T(8,128)(2,1)}, u32[]{:S(2)}) copy-start(bf16[128,128]{1,0:T(8,128)(2,1)} %w_gate.3) | copy-start | bytes 98308
  41.1 14.7 %copy-start.5 = (bf16[32,8,128]{2,1,0:T(8,128)(2,1)S(1)}, bf16[32,8,128]{2,1,0:T(8,128)(2,1)}, u32[]{:S(2)}) copy-start(bf16[32,8,128]{2,1,0:T(8,128)(2,1)} %cotangent.1) | copy-start | bytes 196612
  41.1 14.7 %copy-start.6 = (bf16[128,128]{1,0:T(8,128)(2,1)S(1)}, bf16[128,128]{1,0:T(8,128)(2,1)}, u32[]{:S(2)}) copy-start(bf16[128,128]{1,0:T(8,128)(2,1)} %w_out.1) | copy-start | bytes 98308
  55.8 0.7 copy-start.8
  82.4 14.5 %copy-start.1 = (bf16[128,512]{1,0:T(8,128)(2,1)S(1)}, bf16[128,512]{1,0:T(8,128)(2,1)}, u32[]{:S(2)}) copy-start(bf16[128,512]{1,0:T(8,128)(2,1)} %w_ab.3) | copy-start | bytes 393220
  82.4 14.5 %copy-start.3 = (bf16[32,8,128]{2,1,0:T(8,128)(2,1)S(1)}, bf16[32,8,128]{2,1,0:T(8,128)(2,1)}, u32[]{:S(2)}) copy-start(bf16[32,8,128]{2,1,0:T(8,128)(2,1)} %pair.3) | copy-start | bytes 196612

commit v2 on v1

--- a/solution.py
+++ b/solution.py
@@ -13,6 +13,9 @@
 PAIRS = ROWS * COLS
 GROUP = WIDTH // NCOL
 RES = 256
+SHARE = 3 * COLS
+FINAL = 2 * COLS + SHARE
+GATHER = (16, 8, 4, 2, 1)
 
 
 def dot(left, right, left_dim, right_dim):
@@ -125,16 +128,40 @@
     return wide[:, :COLS].reshape(PAIRS, WIDTH), wide[:, COLS:].reshape(PAIRS, WIDTH)
 
 
-def project_kernel(pair, mask, gain, w_ab, normed_out, send, rows, weights, message):
-    values = load_pairs(pair, rows)
-    h_in, _ = layer_norm(values, 1)
-    normed = (h_in * gain[...]).astype(BF16)
+def project_kernel(
+    pair, mask, gain, w_ab, gain_out, normed_out, wide_out, send, gain_out_kept,
+    pair_here, mask_here, gain_here, w_here, rows, weights, message, sems,
+):
+    copies = [
+        pltpu.make_async_copy(there, here, sems.at[place])
+        for place, (there, here) in enumerate(
+            (
+                (pair, pair_here),
+                (mask, mask_here),
+                (gain, gain_here),
+                (w_ab, w_here),
+                (gain_out, gain_out_kept),
+            )
+        )
+    ]
+    for copy in copies:
+        copy.start()
+    for copy in copies:
+        copy.wait()
+    h_in, _ = layer_norm(pair_here[...].astype(F32).reshape(PAIRS, WIDTH), 1)
+    rows[...] = (h_in * gain_here[...]).astype(BF16).astype(F32)
+    normed = jnp.concatenate(
+        [rows[pl.ds(k, ROWS, stride=COLS), :] for k in range(COLS)], axis=0
+    ).astype(BF16)
     normed_out[...] = normed
-    weights[...] = w_ab[...].astype(F32).T
+    flags = mask_rows(mask_here)
+    wide_out[...] = jnp.concatenate(
+        [rows[i * COLS : (i + 1) * COLS] * flags[:, i : i + 1] for i in range(ROWS)], axis=1
+    ).astype(BF16)
+    weights[...] = w_here[...].astype(F32).T
     proj = dot(regroup(weights, 4).astype(BF16), normed, 1, 1)
     a_val = jax.nn.sigmoid(proj[0:128]) * proj[128:256]
     b_val = jax.nn.sigmoid(proj[256:384]) * proj[384:512]
-    flags = mask_rows(mask)
     for k in range(COLS):
         flag = flags[k : k + 1]
         message[pl.ds(k, NCOL, stride=2 * COLS), :] = to_message(a_val, k) * flag
@@ -155,7 +182,7 @@
 
 def middle_kernel(
     recv, normed_in, cotangent, w_gate, gain, w_out,
-    update, send, d_gate_out, grad_gate, grad_out, rows, weights,
+    update, send, d_gate_out, rows, weights,
 ):
     mixed = from_message([recv[pl.ds(k, NCOL, stride=COLS), :] for k in range(COLS)])
     h_out, inv_out = layer_norm(mixed, 0)
@@ -172,24 +199,27 @@
     d_gate = (cot * y_val * gate * (1.0 - gate)).astype(BF16)
     d_gate_out[...] = d_gate
     ungroup(dot(normed, d_y, 1, 0), weights, 1)
-    grad_out[...] = weights[...]
-    grad_gate[...] = dot(flat_in, d_gate, 0, 0)
     grad_h = dot(w_own, d_y, 1, 1) * scale
     d_mixed = norm_back(grad_h, h_out, inv_out, 0)
     for k in range(COLS):
         rows[pl.ds(k, NCOL, stride=COLS), :] = to_message(d_mixed, k)
-    send[...] = rows[...].astype(BF16)
-
-
-def grad_kernel(recv, b_all, d_mixed, d_a, d_b):
+    sums = jnp.concatenate([dot(flat_in, d_gate, 0, 0), weights[...]], axis=0)
+    both = jnp.concatenate(
+        [rows[...].reshape(NCOL, COLS, WIDTH), sums.reshape(NCOL, COLS, WIDTH)], axis=1
+    )
+    send[...] = both.reshape(2 * PAIRS, WIDTH).astype(BF16)
+
+
+def grad_kernel(recv, b_all, recv_d, d_a, d_b):
     a_val = halves(recv[...])[0].astype(BF16)
+    d_mixed = halves(recv_d[...])[0]
     own = (
         lax.broadcasted_iota(jnp.int32, (WIDTH, WIDTH), 0) // ROWS
         == lane_block((WIDTH, WIDTH))
     )
     total = None
     for r in range(NROW):
-        part = d_mixed[r * ROWS : (r + 1) * ROWS].astype(F32)
+        part = d_mixed[r * ROWS : (r + 1) * ROWS]
         spread = jnp.where(own, jnp.concatenate([part] * GROUP, axis=0), 0.0).astype(BF16)
         term = dot(b_all[r * RES : (r + 1) * RES], spread, 1, 0)
         total = term if total is None else total + term
@@ -197,19 +227,75 @@
     d_a[...] = total
 
 
-def join_kernel(d_a, d_b, send):
+def in_gather_order(values, col):
+    for bit in range(5):
+        size = COLS << bit
+        pairs = values.reshape(RES // (2 * size), 2, size, WIDTH)
+        swapped = jnp.concatenate([pairs[:, 1:], pairs[:, :1]], axis=1)
+        values = jnp.where((col >> bit) & 1 == 1, swapped, pairs).reshape(RES, WIDTH)
+    places = [0]
+    for step in GATHER:
+        places += [place ^ step for place in places]
+    return jnp.concatenate([values[p * COLS : (p + 1) * COLS] for p in places], axis=0)
+
+
+def weight_kernel(
+    col, wide_0, wide_1, w_ab, d_a, d_b, recv_d, d_b_sum, send, proj, d_proj
+):
     total = d_b[0:RES].astype(F32)
     for r in range(1, NROW):
         total = total + d_b[r * RES : (r + 1) * RES].astype(F32)
-    both = jnp.concatenate(
-        [d_a[...].reshape(NCOL, COLS, WIDTH), total.reshape(NCOL, COLS, WIDTH)], axis=1
-    )
-    send[...] = both.reshape(2 * PAIRS, WIDTH).astype(BF16)
+    d_b_sum[...] = total
+    taps = 4 * GROUP
+    tall = 4 * WIDTH
+    tap = lax.broadcasted_iota(jnp.int32, (tall, taps), 1)
+    source = tap // GROUP * WIDTH + col[0] * GROUP + tap % GROUP
+    pick = (lax.broadcasted_iota(jnp.int32, (tall, taps), 0) == source).astype(F32)
+    w_own = dot(pick.astype(BF16), w_ab[...], 0, 1).astype(BF16)
+    sides = (wide_0, wide_1)
+    for side, wide in enumerate(sides):
+        for i in range(ROWS):
+            part = wide[:, i * WIDTH : (i + 1) * WIDTH]
+            proj[pl.ds(side * tall + i, taps, stride=ROWS), :] = dot(w_own, part, 1, 1)
+    for half, d_val in enumerate((d_a[...], total)):
+        turned = in_gather_order(d_val, col[0]).T
+        for side in range(2):
+            start = side * tall + half * 2 * WIDTH
+            sig = jax.nn.sigmoid(proj[start : start + WIDTH])
+            value = proj[start + WIDTH : start + 2 * WIDTH]
+            d_value = turned[:, side * WIDTH : (side + 1) * WIDTH] * sig
+            d_proj[start : start + WIDTH] = d_value * value * (1.0 - sig)
+            d_proj[start + WIDTH : start + 2 * WIDTH] = d_value
+    sums = None
+    for side, wide in enumerate(sides):
+        for i in range(ROWS):
+            left = d_proj[pl.ds(side * tall + i, taps, stride=ROWS), :].astype(BF16)
+            term = dot(left, wide[:, i * WIDTH : (i + 1) * WIDTH], 1, 0)
+            sums = term if sums is None else sums + term
+    share = jnp.sum(recv_d[...].astype(F32).reshape(NCOL, 2 * COLS, WIDTH)[:, COLS:], axis=0)
+    own = jnp.concatenate([sums, share], axis=0) * (1.0 / RES)
+    for r in range(NROW):
+        send[r * SHARE : (r + 1) * SHARE] = own
+
+
+def join_kernel(d_a, d_b, sums, send):
+    total = sums[0:SHARE]
+    for r in range(1, NROW):
+        total = total + sums[r * SHARE : (r + 1) * SHARE]
+    everything = jnp.concatenate(
+        [
+            d_a[...].reshape(NCOL, COLS, WIDTH),
+            d_b[...].reshape(NCOL, COLS, WIDTH),
+            jnp.broadcast_to(total[None], (NCOL, SHARE, WIDTH)),
+        ],
+        axis=1,
+    )
+    send[...] = everything.reshape(NCOL * FINAL, WIDTH).astype(BF16)
 
 
 def last_kernel(
     recv, pair, mask, gain, w_ab, w_gate, normed_in, d_gate,
-    grad_pair, grad_ab, rows, weights, message,
+    grad_pair, grad_ab, grad_gate, grad_out, rows, weights, message,
 ):
     values = load_pairs(pair, rows)
     h_in, inv_in = layer_norm(values, 1)
@@ -222,7 +308,7 @@
     grads = []
     for half in range(2):
         pieces = [
-            message[pl.ds(half * COLS + k, NCOL, stride=2 * COLS), :] * flags[k : k + 1]
+            message[pl.ds(half * COLS + k, NCOL, stride=FINAL), :] * flags[k : k + 1]
             for k in range(COLS)
         ]
         d_val = from_message(pieces)
@@ -233,69 +319,107 @@
     d_proj = jnp.concatenate(grads, axis=0).astype(BF16)
     d_in = dot(d_proj, w_own, 0, 0) + dot(d_gate[...], w_gate[...], 1, 1)
     store_pairs(norm_back(d_in * gain[...], h_in, inv_in, 1), rows, grad_pair)
-    ungroup(dot(d_proj, flat_in, 1, 0), weights, 4)
-    grad_ab[...] = weights[...]
-
-
-def call(kernel, outs, scratch, *args):
+    for blk in range(4):
+        for c4 in range(GROUP):
+            weights[pl.ds(blk * WIDTH + c4, NCOL, stride=GROUP), :] = message[
+                pl.ds(2 * COLS + blk * GROUP + c4, NCOL, stride=FINAL), :
+            ]
+    grad_ab[...] = weights[...].T
+    others = message[...].reshape(NCOL, FINAL, WIDTH)[:, FINAL - COLS :].reshape(PAIRS, WIDTH)
+    grad_gate[...] = others[:WIDTH]
+    grad_out[...] = others[WIDTH:]
+
+
+def call(kernel, outs, scratch, *args, places=None):
     return pl.pallas_call(
         kernel,
         out_shape=[jax.ShapeDtypeStruct(shape, dtype) for shape, dtype in outs],
-        scratch_shapes=[pltpu.VMEM(shape, F32) for shape in scratch],
+        in_specs=[
+            pl.BlockSpec(memory_space=pltpu.VMEM if places is None else places[n])
+            for n in range(len(args))
+        ],
+        scratch_shapes=scratch,
         compiler_params=pltpu.CompilerParams(vmem_limit_bytes=32 * 1024 * 1024),
     )(*args)
 
 
 def exchange(values, axis):
     return lax.all_to_all(values, axis, 0, 0, tiled=True)
+
+
+def beside(values, axis, held, step):
+    values, held = lax.optimization_barrier((values, held))
+    came = lax.ppermute(held, "col", [(col, col ^ step) for col in range(NCOL)])
+    return lax.optimization_barrier((exchange(values, axis), held, came))
 
 
 def on_device(pair, pair_mask, ln_in_gain, w_ab, w_gate, ln_out_gain, w_out, cotangent):
     gain_in = ln_in_gain.reshape(1, WIDTH)
     gain_out = ln_out_gain.reshape(1, WIDTH)
+    col = lax.axis_index("col").astype(jnp.int32).reshape(1)
     flat = (PAIRS, WIDTH)
     twice = (2 * PAIRS, WIDTH)
     copies = (NROW * RES, WIDTH)
     blocks = (ROWS, COLS, WIDTH)
-    normed_in, send_ab = call(
+    square = (WIDTH, WIDTH)
+    wide = (WIDTH, 4 * WIDTH)
+    tall = (4 * WIDTH, WIDTH)
+    normed_in, wide_in, send_ab, gain_out = call(
         project_kernel,
-        [(flat, BF16), (twice, BF16)],
-        [flat, (4 * WIDTH, WIDTH), twice],
-        pair, pair_mask, gain_in, w_ab,
-    )
-    recv_ab = exchange(send_ab, "col")
+        [(flat, BF16), ((COLS, ROWS * WIDTH), BF16), (twice, BF16), ((1, WIDTH), F32)],
+        [
+            pltpu.VMEM(blocks, BF16),
+            pltpu.VMEM((ROWS, COLS), jnp.int32),
+            pltpu.VMEM((1, WIDTH), F32),
+            pltpu.VMEM(wide, BF16),
+            pltpu.VMEM(flat, F32),
+            pltpu.VMEM(tall, F32),
+            pltpu.VMEM(twice, F32),
+            pltpu.SemaphoreType.DMA((5,)),
+        ],
+        pair, pair_mask, gain_in, w_ab, gain_out,
+        places=[pltpu.HBM] * 5,
+    )
+    recv_ab, held, came = beside(send_ab, "col", wide_in, GATHER[0])
+    held = jnp.concatenate([held, came], axis=0)
     b_own = recv_ab.reshape(NCOL, 2 * COLS, WIDTH)[:, COLS:].reshape(flat)
-    b_all = exchange(jnp.broadcast_to(b_own[None], (NROW,) + flat).reshape(copies), "row")
+    copied = jnp.broadcast_to(b_own[None], (NROW,) + flat).reshape(copies)
+    b_all, held, came = beside(copied, "row", held, GATHER[1])
+    held = jnp.concatenate([held, came], axis=0)
     (send_mixed,) = call(mix_kernel, [(flat, F32)], [], recv_ab, b_all)
-    recv_mixed = exchange(send_mixed, "col")
-    update, send_d, d_gate, grad_gate, grad_out = call(
+    recv_mixed, held, came = beside(send_mixed, "col", held, GATHER[2])
+    held = jnp.concatenate([held, came], axis=0)
+    update, send_d, d_gate = call(
         middle_kernel,
-        [(blocks, BF16), (flat, BF16), (flat, BF16), ((WIDTH, WIDTH), F32), ((WIDTH, WIDTH), F32)],
-        [flat, (WIDTH, WIDTH)],
+        [(blocks, BF16), (twice, BF16), (flat, BF16)],
+        [pltpu.VMEM(flat, F32), pltpu.VMEM(square, F32)],
         recv_mixed, normed_in, cotangent, w_gate, gain_out, w_out,
     )
-    d_mixed = exchange(send_d, "col")
-    d_a, d_b = call(grad_kernel, [(flat, F32), (copies, BF16)], [], recv_ab, b_all, d_mixed)
-    d_b = exchange(d_b, "row")
-    (send_grads,) = call(join_kernel, [(twice, BF16)], [], d_a, d_b)
-    recv_grads = exchange(send_grads, "col")
-    grad_pair, grad_ab = call(
+    recv_d, held, came = beside(send_d, "col", held, GATHER[3])
+    held = jnp.concatenate([held, came], axis=0)
+    d_a, d_b = call(grad_kernel, [(flat, F32), (copies, BF16)], [], recv_ab, b_all, recv_d)
+    d_b, held, came = beside(d_b, "row", held, GATHER[4])
+    d_b, sums = call(
+        weight_kernel,
+        [(flat, F32), ((NROW * SHARE, WIDTH), F32)],
+        [pltpu.VMEM((8 * WIDTH, WIDTH), F32), pltpu.VMEM((8 * WIDTH, WIDTH), F32)],
+        col, held, came, w_ab, d_a, d_b, recv_d,
+        places=[pltpu.SMEM] + [pltpu.VMEM] * 6,
+    )
+    sums = exchange(sums, "row")
+    (send_last,) = call(join_kernel, [((NCOL * FINAL, WIDTH), BF16)], [], d_a, d_b, sums)
+    recv_last = exchange(send_last, "col")
+    return call(
         last_kernel,
-        [(blocks, BF16), ((4 * WIDTH, WIDTH), F32)],
-        [flat, (4 * WIDTH, WIDTH), twice],
-        recv_grads, pair, pair_mask, gain_in, w_ab, w_gate, normed_in, d_gate,
-    )
-    both = ("row", "col")
-    local = jnp.concatenate([grad_ab, grad_gate, grad_out], axis=0).reshape(RES, 1, 3 * WIDTH)
-    own = jnp.sum(exchange(local, both), axis=0, keepdims=True)
-    total = exchange(jnp.broadcast_to(own, local.shape), both).reshape(6 * WIDTH, WIDTH) / RES
-    return (
-        update,
-        grad_pair,
-        total[: 4 * WIDTH].T,
-        total[4 * WIDTH : 5 * WIDTH],
-        total[5 * WIDTH :],
-    )
+        [(blocks, BF16), (wide, F32), (square, F32), (square, F32)],
+        [pltpu.VMEM(flat, F32), pltpu.VMEM(tall, F32), pltpu.VMEM((NCOL * FINAL, WIDTH), F32)],
+        recv_last, pair, pair_mask, gain_in, w_ab, w_gate, normed_in, d_gate,
+    ), update
+
+
+def all_outputs(*args):
+    (grad_pair, grad_ab, grad_gate, grad_out), update = on_device(*args)
+    return update, grad_pair, grad_ab, grad_gate, grad_out
 
 
 def solution(mesh):
@@ -310,7 +434,7 @@
         P("row", "col", None),
     )
     return jax.shard_map(
-        on_device,
+        all_outputs,
         mesh=mesh,
         in_specs=placed,
         out_specs=(P("row", "col", None), P("row", "col", None), P(), P(), P()),

time: 148 us -> 129 us (0.87)
  blocking collectives: 136 us -> 58.2 us
  starting transfers between devices: 0 us -> 28.8 us
  waiting for transfers between devices: 0 us -> 27.2 us
  Pallas kernels: 4.44 us -> 8.72 us
    all_to_all x8 -> x4, blocking collectives: 136 us -> 58.2 us  [exchange(): return lax.all_to_all(values, axis, 0, 0, tiled=True)]
    all_to_all x0 -> x3, starting transfers between devices: none -> 21.9 us  [exchange(): return lax.all_to_all(values, axis, 0, 0, tiled=True)]
    ppermute x0 -> x5, waiting for transfers between devices: none -> 15.6 us  [beside(): came = lax.ppermute(held, 'col', [(col, col ^ step) for col in range(NCOL)])]
    all_to_all x0 -> x3, waiting for transfers between devices: none -> 11.6 us  [exchange(): return lax.all_to_all(values, axis, 0, 0, tiled=True)]
    ppermute x0 -> x5, starting transfers between devices: none -> 6.84 us  [beside(): came = lax.ppermute(held, 'col', [(col, col ^ step) for col in range(NCOL)])]
    pallas_call x6 -> x7, Pallas kernels: 4.44 us -> 8.72 us  [call(): pl.pallas_call(kernel, out_shape=[jax.ShapeDtypeStruct(shape, dtype) for...]
    unnamed x20 -> x21, local copies, waits for them, and re-layouts: 4.67 us -> 3.85 us
  transfers between devices with their start and end apart: 0 -> 8, of which waited for: 0 -> 4; matrix products, arithmetic and copies ran while one was open for 0% -> 0% of each run, Pallas kernels for 0% -> 0%
where the time goes in v2:
time: 129 us
  blocking collectives  58.2 us (45%)
  starting transfers between devices  28.8 us (22%)
  waiting for transfers between devices  27.2 us (21%)
  Pallas kernels  8.72 us (7%)
  local copies, waits for them, and re-layouts  4.73 us (4%)
    all_to_all x4, blocking collectives, exchange(): return lax.all_to_all(values, axis, 0, 0, tiled=True)  58.2 us
    all_to_all x3, starting transfers between devices, exchange(): return lax.all_to_all(values, axis, 0, 0, tiled=True)  21.9 us
    ppermute x5, waiting for transfers between devices, beside(): came = lax.ppermute(held, 'col', [(col, col ^ step) for col in range(NCOL)])  15.6 us
    all_to_all x3, waiting for transfers between devices, exchange(): return lax.all_to_all(values, axis, 0, 0, tiled=True)  11.6 us
    pallas_call x7, Pallas kernels, call(): pl.pallas_call(kernel, out_shape=[jax.ShapeDtypeStruct(shape, dtype) for...  8.72 us
    ppermute x5, starting transfers between devices, beside(): came = lax.ppermute(held, 'col', [(col, col ^ step) for col in range(NCOL)])  6.84 us
    unnamed x21, local copies, waits for them, and re-layouts  3.85 us
  transfers between devices with their start and end apart: 8, of which 4 were waited for; matrix products, arithmetic and copies ran while one was open for 0% of the time, Pallas kernels for 0%

profile of v2, /device:TPU:1, one launch (start us, length us, event | category | flops | bytes accessed | tf_op | source)
XLA Modules:
  0.0 128.6 jit_solution(11956731969206127000)
XLA Ops:
  0.6 0.8 copy.13.mask
  1.4 0.0 copy-start
  1.4 0.9 copy-done
  2.3 0.0 copy-start.2
  2.3 0.8 copy-done.2
  3.1 0.0 copy-start.7
  3.1 0.7 copy-done.7
  3.8 0.0 copy-start.9
  3.8 0.7 copy-done.9
  4.5 1.7 %shard_map.119 = (bf16[256,128]{1,0:T(8,128)(2,1)S(1)}, bf16[8,4096]{1,0:T(8,128)(2,1)S(1)}, bf16[512,128]{1,0:T(8,128)(2,1)}, f32[1,128]{1,0:T(1,128)S(1)}) custom-call(bf16[32,8,128]{2,1,0:T(8,128)(2,1)S(1)} %copy-done.2, s32[32,8]{1,0:T(8,128)S(1)} %copy.13.mask, f32[1,128]{1,0:T(1,128)S(1)} %bitcast.35, bf16[128,512]{1,0:T(8,128)(2,1)S(1)} %copy-done, ...), custom_call_target="tpu_custom_call" | custom-call | tf_op jit(solution)/shard_map/pallas_call | solution.py:334
  6.2 11.2 %all-to-all-start = ((bf16[32,16,128]{2,1,0:T(8,128)(2,1)}), bf16[32,16,128]{2,1,0:T(8,128)(2,1)S(1)}, u32[]{:S(2)}, u32[]{:S(2)}) async-start(bf16[32,16,128]{2,1,0:T(8,128)(2,1)} %bitcast.2), calls=%async_computation | async-start | bytes 262144 | tf_op jit(solution)/shard_map/all_to_all | solution.py:347
  17.3 5.4 %collective-permute-start = (bf16[8,4096]{1,0:T(8,128)(2,1)S(1)}, bf16[8,4096]{1,0:T(8,128)(2,1)S(1)}, u32[]{:S(2)}, u32[]{:S(2)}) collective-permute-start(bf16[8,4096]{1,0:T(8,128)(2,1)S(1)} %get-tuple-element.50), channel_id=1, source_target_pairs={{0,16},{1,17},{2,18},{3,19},{4,20},{5,21},{6,22},{7,23},{8,24},{9,... | collective-permute-start | bytes 196616 | tf_op jit(solution)/shard_map/ppermute | solution.py:352
  22.7 6.5 %collective-permute-done = bf16[8,4096]{1,0:T(8,128)(2,1)S(1)} collective-permute-done((bf16[8,4096]{1,0:T(8,128)(2,1)S(1)}, bf16[8,4096]{1,0:T(8,128)(2,1)S(1)}, u32[]{:S(2)}, u32[]{:S(2)}) %collective-permute-start) | collective-permute-done | bytes 65568 | tf_op jit(solution)/shard_map/ppermute | solution.py:352
  29.3 0.0 all-to-all-done
  29.3 0.9 broadcast_in_dim.8
  30.2 6.4 %all-to-all-start.1 = ((bf16[8,256,128]{2,1,0:T(8,128)(2,1)}), bf16[8,256,128]{2,1,0:T(8,128)(2,1)S(1)}, u32[]{:S(2)}, u32[]{:S(2)}) async-start(bf16[8,256,128]{2,1,0:T(8,128)(2,1)} %bitcast.7), calls=%async_computation.1 | async-start | bytes 1048576 | tf_op jit(solution)/shard_map/all_to_all | solution.py:347
  36.5 0.0 collective-permute-start.1
  36.5 9.1 %collective-permute-done.1 = bf16[16,4096]{1,0:T(8,128)(2,1)S(1)} collective-permute-done((bf16[16,4096]{1,0:T(8,128)(2,1)S(1)}, bf16[16,4096]{1,0:T(8,128)(2,1)S(1)}, u32[]{:S(2)}, u32[]{:S(2)}) %collective-permute-start.1) | collective-permute-done | bytes 131104 | tf_op jit(solution)/shard_map/ppermute | solution.py:352
  45.6 1.1 all-to-all-done.1
  46.7 0.3 shard_map.120
  47.1 0.0 copy-start.4
  47.1 0.0 copy-start.5
  47.1 0.0 copy-start.6
  47.1 0.4 collective-permute-start.2
  47.5 15.5 %all_to_all.82 = f32[32,8,128]{2,1,0:T(8,128)S(1)} all-to-all(f32[32,8,128]{2,1,0:T(8,128)S(1)} %bitcast.31), channel_id=1, replica_groups=mesh['row'=8,'col'=32] {'col'}, dimensions={0} | all-to-all | bytes 262144 | tf_op jit(solution)/shard_map/all_to_all | solution.py:347
  63.1 0.0 collective-permute-done.2
  63.1 0.0 copy-done.4
  63.1 0.0 copy-done.5
  63.1 0.0 copy-done.6
  63.1 1.4 %shard_map.121 = (bf16[32,8,128]{2,1,0:T(8,128)(2,1)}, bf16[512,128]{1,0:T(8,128)(2,1)S(1)}, bf16[256,128]{1,0:T(8,128)(2,1)S(1)}) custom-call(f32[256,128]{1,0:T(8,128)S(1)} %bitcast.30, bf16[256,128]{1,0:T(8,128)(2,1)S(1)} %get-tuple-element.60.normed_in, bf16[32,8,128]{2,1,0:T(8,128)(2,1)S(1)} %copy-done.5, bf16[128,128]{1,0:T(8,128)(2,1)S(1)} %copy-done.4, ...), custom_call_target="tpu_custom_call" | custom-call | tf_op jit(solution)/shard_map/pallas_call | solution.py:334
  64.6 0.6 collective-permute-start.3
  65.2 14.7 %all_to_all.83 = bf16[32,16,128]{2,1,0:T(8,128)(2,1)S(1)} all-to-all(bf16[32,16,128]{2,1,0:T(8,128)(2,1)S(1)} %bitcast.33), channel_id=1, replica_groups=mesh['row'=8,'col'=32] {'col'}, dimensions={0} | all-to-all | bytes 262144 | tf_op jit(solution)/shard_map/all_to_all | solution.py:347
  79.9 0.0 collective-permute-done.3
  79.9 1.2 shard_map.122
  81.1 0.1 pad_maximum_fusion.wide_0
  81.2 0.0 copy-start.1
  81.2 0.5 collective-permute-start.4
  81.7 4.4 %all-to-all-start.4 = ((bf16[8,256,128]{2,1,0:T(8,128)(2,1)}), bf16[8,256,128]{2,1,0:T(8,128)(2,1)S(1)}, u32[]{:S(2)}, u32[]{:S(2)}) async-start(bf16[8,256,128]{2,1,0:T(8,128)(2,1)} %bitcast.14), calls=%async_computation.4 | async-start | bytes 1048576 | tf_op jit(solution)/shard_map/all_to_all | solution.py:347
  86.2 10.5 %all-to-all-done.4 = bf16[8,256,128]{2,1,0:T(8,128)(2,1)S(1)} async-done(((bf16[8,256,128]{2,1,0:T(8,128)(2,1)}), bf16[8,256,128]{2,1,0:T(8,128)(2,1)S(1)}, u32[]{:S(2)}, u32[]{:S(2)}) %all-to-all-start.4) | async-done | bytes 524320 | tf_op jit(solution)/shard_map/all_to_all | solution.py:347
  96.7 0.0 collective-permute-done.4.wide_1
  96.7 0.0 copy-done.1
  96.7 2.3 %shard_map.123 = (f32[256,128]{1,0:T(8,128)S(1)}, f32[192,128]{1,0:T(8,128)S(1)}) custom-call(s32[1]{0:T(128)} %bitcast.13.col, bf16[128,4096]{1,0:T(8,128)(2,1)S(1)} %pad_maximum_fusion.wide_0, bf16[128,4096]{1,0:T(8,128)(2,1)S(1)} %collective-permute-done.4.wide_1, bf16[128,512]{1,0:T(8,128)(2,1)S(1)} %copy-done.1, f32[256,128]{1,0:T(8,128)S(1)} %get-tuple-element.69.d_a, ...), custom_call_target="tpu_custom_call" | custom-call | tf_op jit(solution)/shard_map/pallas_call | solution.py:334
  99.0 0.0 copy-start.3
  99.0 0.0 copy-start.8
  99.0 10.0 %all_to_all.84 = f32[8,24,128]{2,1,0:T(8,128)S(1)} all-to-all(f32[8,24,128]{2,1,0:T(8,128)S(1)} %bitcast.34), channel_id=1, replica_groups=mesh['row'=8,'col'=32] {'row'}, dimensions={0} | all-to-all | bytes 196608 | tf_op jit(solution)/shard_map/all_to_all | solution.py:347
  109.0 17.9 %all_to_all.85 = bf16[32,40,128]{2,1,0:T(8,128)(2,1)S(1)} all-to-all(bf16[32,40,128]{2,1,0:T(8,128)(2,1)S(1)} %bitcast.27), channel_id=1, replica_groups=mesh['row'=8,'col'=32] {'col'}, dimensions={0} | all-to-all | bytes 655360 | tf_op jit(solution)/shard_map/all_to_all | solution.py:347
  127.0 0.0 copy-done.3
  127.0 0.0 copy-done.8
  127.0 1.7 %shard_map.125 = (bf16[32,8,128]{2,1,0:T(8,128)(2,1)}, f32[128,512]{1,0:T(8,128)}, f32[128,128]{1,0:T(8,128)}, f32[128,128]{1,0:T(8,128)}) custom-call(bf16[1280,128]{1,0:T(8,128)(2,1)S(1)} %bitcast.26, bf16[32,8,128]{2,1,0:T(8,128)(2,1)S(1)} %copy-done.3, s32[32,8]{1,0:T(8,128)S(1)} %copy.13.mask, f32[1,128]{1,0:T(1,128)S(1)} %bitcast.36, ...), custom_call_target="tpu_custom_call" | custom-call | tf_op jit(solution)/shard_map/pallas_call | solution.py:334
  (5 shorter events, 0.1 us)
Async XLA Ops:
  1.4 0.9 copy-start
  2.3 0.8 copy-start.2
  3.1 0.7 copy-start.7
  3.8 0.7 copy-start.9
  6.2 23.1 %all-to-all-start = ((bf16[32,16,128]{2,1,0:T(8,128)(2,1)}), bf16[32,16,128]{2,1,0:T(8,128)(2,1)S(1)}, u32[]{:S(2)}, u32[]{:S(2)}) async-start(bf16[32,16,128]{2,1,0:T(8,128)(2,1)} %bitcast.2), calls=%async_computation | async-start | bytes 262144 | tf_op jit(solution)/shard_map/all_to_all | solution.py:347
  17.3 11.9 %collective-permute-start = (bf16[8,4096]{1,0:T(8,128)(2,1)S(1)}, bf16[8,4096]{1,0:T(8,128)(2,1)S(1)}, u32[]{:S(2)}, u32[]{:S(2)}) collective-permute-start(bf16[8,4096]{1,0:T(8,128)(2,1)S(1)} %get-tuple-element.50), channel_id=1, source_target_pairs={{0,16},{1,17},{2,18},{3,19},{4,20},{5,21},{6,22},{7,23},{8,24},{9,... | collective-permute-start | bytes 196616 | tf_op jit(solution)/shard_map/ppermute | solution.py:352
  30.2 16.5 %all-to-all-start.1 = ((bf16[8,256,128]{2,1,0:T(8,128)(2,1)}), bf16[8,256,128]{2,1,0:T(8,128)(2,1)S(1)}, u32[]{:S(2)}, u32[]{:S(2)}) async-start(bf16[8,256,128]{2,1,0:T(8,128)(2,1)} %bitcast.7), calls=%async_computation.1 | async-start | bytes 1048576 | tf_op jit(solution)/shard_map/all_to_all | solution.py:347
  36.5 9.1 %collective-permute-start.1 = (bf16[16,4096]{1,0:T(8,128)(2,1)S(1)}, bf16[16,4096]{1,0:T(8,128)(2,1)S(1)}, u32[]{:S(2)}, u32[]{:S(2)}) collective-permute-start(bf16[16,4096]{1,0:T(8,128)(2,1)S(1)} %pad_maximum_fusion.3), channel_id=1, source_target_pairs={{0,8},{1,9},{2,10},{3,11},{4,12},{5,13},{6,14},{7,15},{8,0},{9,1},... | collective-permute-start | bytes 393224 | tf_op jit(solution)/shard_map/ppermute | solution.py:352
  47.1 16.1 %copy-start.4 = (bf16[128,128]{1,0:T(8,128)(2,1)S(1)}, bf16[128,128]{1,0:T(8,128)(2,1)}, u32[]{:S(2)}) copy-start(bf16[128,128]{1,0:T(8,128)(2,1)} %w_gate.3) | copy-start | bytes 98308
  47.1 16.1 %copy-start.5 = (bf16[32,8,128]{2,1,0:T(8,128)(2,1)S(1)}, bf16[32,8,128]{2,1,0:T(8,128)(2,1)}, u32[]{:S(2)}) copy-start(bf16[32,8,128]{2,1,0:T(8,128)(2,1)} %cotangent.1) | copy-start | bytes 196612
  47.1 16.1 %copy-start.6 = (bf16[128,128]{1,0:T(8,128)(2,1)S(1)}, bf16[128,128]{1,0:T(8,128)(2,1)}, u32[]{:S(2)}) copy-start(bf16[128,128]{1,0:T(8,128)(2,1)} %w_out.1) | copy-start | bytes 98308
  47.1 16.0 %collective-permute-start.2 = (bf16[32,4096]{1,0:T(8,128)(2,1)S(1)}, bf16[32,4096]{1,0:T(8,128)(2,1)S(1)}, u32[]{:S(2)}, u32[]{:S(2)}) collective-permute-start(bf16[32,4096]{1,0:T(8,128)(2,1)S(1)} %pad_maximum_fusion.2), channel_id=1, source_target_pairs={{0,4},{1,5},{2,6},{3,7},{4,0},{5,1},{6,2},{7,3},{8,12},{9,13},{10,... | collective-permute-start | bytes 786440 | tf_op jit(solution)/shard_map/ppermute | solution.py:352
  64.6 15.3 %collective-permute-start.3 = (bf16[64,4096]{1,0:T(8,128)(2,1)S(1)}, bf16[64,4096]{1,0:T(8,128)(2,1)S(1)}, u32[]{:S(2)}, u32[]{:S(2)}) collective-permute-start(bf16[64,4096]{1,0:T(8,128)(2,1)S(1)} %pad_maximum_fusion.1), channel_id=1, source_target_pairs={{0,2},{1,3},{2,0},{3,1},{4,6},{5,7},{6,4},{7,5},{8,10},{9,11},{10,... | collective-permute-start | bytes 1572872 | tf_op jit(solution)/shard_map/ppermute | solution.py:352
  81.2 15.5 %copy-start.1 = (bf16[128,512]{1,0:T(8,128)(2,1)S(1)}, bf16[128,512]{1,0:T(8,128)(2,1)}, u32[]{:S(2)}) copy-start(bf16[128,512]{1,0:T(8,128)(2,1)} %w_ab.5) | copy-start | bytes 393220
  81.2 15.4 %collective-permute-start.4 = (bf16[128,4096]{1,0:T(8,128)(2,1)S(1)}, bf16[128,4096]{1,0:T(8,128)(2,1)S(1)}, u32[]{:S(2)}, u32[]{:S(2)}) collective-permute-start(bf16[128,4096]{1,0:T(8,128)(2,1)S(1)} %pad_maximum_fusion.wide_0), channel_id=1, source_target_pairs={{0,1},{1,0},{2,3},{3,2},{4,5},{5,4},{6,7},{7,6},{8,9},{9,8},{10,11... | collective-permute-start | bytes 3145736 | tf_op jit(solution)/shard_map/ppermute | solution.py:352
  81.7 14.9 %all-to-all-start.4 = ((bf16[8,256,128]{2,1,0:T(8,128)(2,1)}), bf16[8,256,128]{2,1,0:T(8,128)(2,1)S(1)}, u32[]{:S(2)}, u32[]{:S(2)}) async-start(bf16[8,256,128]{2,1,0:T(8,128)(2,1)} %bitcast.14), calls=%async_computation.4 | async-start | bytes 1048576 | tf_op jit(solution)/shard_map/all_to_all | solution.py:347
  99.0 28.0 %copy-start.3 = (bf16[32,8,128]{2,1,0:T(8,128)(2,1)S(1)}, bf16[32,8,128]{2,1,0:T(8,128)(2,1)}, u32[]{:S(2)}) copy-start(bf16[32,8,128]{2,1,0:T(8,128)(2,1)} %pair.3) | copy-start | bytes 196612
  99.0 28.0 %copy-start.8 = (f32[128]{0:T(128)S(1)}, f32[128]{0:T(128)}, u32[]{:S(2)}) copy-start(f32[128]{0:T(128)} %param.10) | copy-start | bytes 1540

commit v3 on v1

v3 whole, which is shorter than its diff:
```python
import jax
import jax.numpy as jnp
from jax import lax
from jax.experimental import pallas as pl
from jax.experimental.pallas import tpu as pltpu
from jax.sharding import Mesh, PartitionSpec as P

F32 = jnp.float32
BF16 = jnp.bfloat16

ROWS, COLS, WIDTH = 32, 8, 128
NROW, NLANE, NSIDE = 8, 16, 16
PAIRS = ROWS * COLS
GROUP = WIDTH // NLANE
QUAD = WIDTH // ROWS
HALF = ROWS // 2
RES = 256
TAPS = 4 * GROUP
SHARE = TAPS + 2 * WIDTH // NLANE
FINAL = 4 * COLS + SHARE
GATHER = (("z", 4), ("z", 2), ("z", 1), ("core", 1))


def dot(left, right, left_dim, right_dim):
    return lax.dot_general(
        left, right, (((left_dim,), (right_dim,)), ((), ())), preferred_element_type=F32
    )


def lane_block(shape, size=ROWS):
    return lax.broadcasted_iota(jnp.int32, shape, 1) // size


def load_pairs(block, scratch):
    scratch[...] = block[...].astype(F32).reshape(PAIRS, WIDTH)
    return jnp.concatenate(
        [scratch[pl.ds(k, ROWS, stride=COLS), :] for k in range(COLS)], axis=0
    )


def store_pairs(values, scratch, block):
    for k in range(COLS):
        scratch[pl.ds(k, ROWS, stride=COLS), :] = values[k * ROWS : (k + 1) * ROWS]
    block[...] = scratch[...].reshape(ROWS, COLS, WIDTH).astype(block.dtype)


def regroup(scratch, blocks):
    return jnp.concatenate(
        [
            scratch[pl.ds(blk * WIDTH + cc, NLANE, stride=GROUP), :]
            for blk in range(blocks)
            for cc in range(GROUP)
        ],
        axis=0,
    )


def ungroup(values, scratch):
    for cc in range(GROUP):
        scratch[pl.ds(cc, NLANE, stride=GROUP), :] = values[cc * NLANE : (cc + 1) * NLANE]


def moved(part, shift):
    shift = shift % WIDTH
    return pltpu.roll(part, shift, 1) if shift else part


def to_message(values, k, which, size):
    tile, start = k // QUAD, k % QUAD * ROWS
    first = which * QUAD
    if size == HALF:
        start, first = start + which * HALF, 0
    block = lane_block((NLANE, WIDTH), size)
    result = None
    for place in range(WIDTH // size):
        row = (first + place) * NLANE
        part = moved(values[row : row + NLANE, tile * WIDTH : (tile + 1) * WIDTH], place * size - start)
        result = part if result is None else jnp.where(block == place, part, result)
    return result


def from_message(pieces, size):
    block = lane_block((NLANE, WIDTH), size)
    bands = []
    for cc in range(GROUP):
        tiles = []
        for tile in range(COLS // QUAD):
            result = None
            for place in range(WIDTH // size):
                if size == ROWS:
                    part = pieces[tile * QUAD + place][cc // QUAD]
                    start = cc % QUAD * ROWS
                else:
                    part = pieces[tile * QUAD + place // 2][place % 2]
                    start = cc * HALF
                part = moved(part, place * size - start)
                result = part if result is None else jnp.where(block == place, part, result)
            tiles.append(result)
        bands.append(jnp.concatenate(tiles, axis=1))
    return jnp.concatenate(bands, axis=0)


def mask_rows(mask):
    flags = mask[...].astype(F32).astype(BF16)
    source = lax.broadcasted_iota(jnp.int32, (ROWS, WIDTH), 0)
    lane = lax.broadcasted_iota(jnp.int32, (ROWS, WIDTH), 1)
    return [
        dot(flags, (place == source).astype(F32).astype(BF16), 1, 0)
        for place in (lane % ROWS, lane % HALF, lane % HALF + HALF)
    ]


def column_of(gain):
    row = lax.broadcasted_iota(jnp.int32, (WIDTH, WIDTH), 0)
    lane = lax.broadcasted_iota(jnp.int32, (WIDTH, WIDTH), 1)
    here = lane == (row % NLANE) * GROUP + row // NLANE
    return jnp.sum(jnp.where(here, gain, 0.0), axis=1, keepdims=True)


def layer_norm(values, axis):
    center = values - jnp.mean(values, axis=axis, keepdims=True)
    inverse = lax.rsqrt(jnp.mean(center * center, axis=axis, keepdims=True) + 1e-05)
    return center * inverse, inverse


def norm_back(grad_h, normed, inverse, axis):
    first = jnp.mean(grad_h, axis=axis, keepdims=True)
    second = jnp.mean(grad_h * normed, axis=axis, keepdims=True)
    return inverse * (grad_h - first - normed * second)


def split_rows(message, parts):
    wide = message.astype(F32).reshape(NLANE, parts, COLS, WIDTH)
    return [wide[:, part].reshape(NLANE * COLS, WIDTH) for part in range(parts)]


def project_kernel(*refs):
    count = len(refs) - 7
    inputs, kept = refs[: count // 2], refs[count // 2 : count]
    normed_out, wide_out, send, rows, weights, message, sems = refs[count:]
    copies = [
        pltpu.make_async_copy(there, here, sems.at[place])
        for place, (there, here) in enumerate(zip(inputs, kept))
    ]
    for copy in copies:
        copy.start()
    for copy in copies:
        copy.wait()
    pair_here, mask_here, gain_here, w_here = kept[:4]
    h_in, _ = layer_norm(pair_here[...].astype(F32).reshape(PAIRS, WIDTH), 1)
    rows[...] = (h_in * gain_here[...]).astype(BF16).astype(F32)
    normed = jnp.concatenate(
        [rows[pl.ds(k, ROWS, stride=COLS), :] for k in range(COLS)], axis=0
    ).astype(BF16)
    normed_out[...] = normed
    flags, *half_flags = mask_rows(mask_here)
    wide_out[...] = jnp.concatenate(
        [rows[i * COLS : (i + 1) * COLS] * flags[:, i : i + 1] for i in range(ROWS)], axis=1
    ).astype(BF16)
    weights[...] = w_here[...].astype(F32).T
    proj = dot(regroup(weights, 4).astype(BF16), normed, 1, 1)
    a_val = jax.nn.sigmoid(proj[0:128]) * proj[128:256]
    b_val = jax.nn.sigmoid(proj[256:384]) * proj[384:512]
    for k in range(COLS):
        for part in range(2):
            message[pl.ds(part * COLS + k, NLANE, stride=4 * COLS), :] = (
                to_message(a_val, k, part, ROWS) * flags[k : k + 1]
            )
            message[pl.ds((2 + part) * COLS + k, NLANE, stride=4 * COLS), :] = (
                to_message(b_val, k, part, HALF) * half_flags[part][k : k + 1]
            )
    send[...] = message[...].astype(BF16)


def spread_kernel(recv, send):
    parts = split_rows(recv[...], 4)
    for side in range(NSIDE):
        send[side * WIDTH : (side + 1) * WIDTH] = parts[2 + side % 2].astype(BF16)


def mix_kernel(recv, recv_near, b_all, send, a_all):
    own, near = split_rows(recv[...], 4), split_rows(recv_near[...], 4)
    is_first = lax.axis_index("y") == 0
    a_val = []
    for first, second in ((own, near), (near, own)):
        a_val.append(
            jnp.concatenate(
                [jnp.where(is_first, first[h], second[h]) for h in range(2)], axis=1
            ).astype(BF16)
        )
    a_all[...] = jnp.concatenate(a_val, axis=0)
    block = lane_block((HALF, WIDTH))
    pieces = []
    for r in range(NROW):
        full = None
        for y in range(2):
            side = 2 * r + y
            term = dot(b_all[side * WIDTH : (side + 1) * WIDTH], a_val[y], 0, 0)
            full = term if full is None else full + term
        found = []
        for h in range(2):
            mixed = None
            for c4 in range(QUAD):
                row = (h * QUAD + c4) * HALF
                part = full[row : row + HALF, h * WIDTH : (h + 1) * WIDTH]
                mixed = part if mixed is None else jnp.where(block == c4, part, mixed)
            found.append(mixed)
        pieces += [found[h][core * COLS : (core + 1) * COLS] for core in range(2) for h in range(2)]
    send[...] = jnp.concatenate(pieces, axis=0).astype(BF16)


def middle_kernel(
    recv, normed_in, cotangent, w_gate, gain, w_out,
    update, send, d_gate_out, rows, weights,
):
    rows[...] = recv[...].astype(F32)
    mixed = from_message(
        [
            [rows[pl.ds(h * COLS + k, NLANE, stride=2 * COLS), :] for h in range(2)]
            for k in range(COLS)
        ],
        ROWS,
    )
    h_out, inv_out = layer_norm(mixed, 0)
    scale = column_of(gain[...])
    normed = (h_out * scale).astype(BF16)
    weights[...] = w_out[...].astype(F32)
    w_own = regroup(weights, 1).astype(BF16)
    y_val = dot(normed, w_own, 0, 0)
    flat_in = normed_in[...]
    gate = jax.nn.sigmoid(dot(flat_in, w_gate[...], 1, 0))
    store_pairs(gate * y_val, rows, update)
    cot = load_pairs(cotangent, rows)
    d_y = (cot * gate).astype(BF16)
    d_gate = (cot * y_val * gate * (1.0 - gate)).astype(BF16)
    d_gate_out[...] = d_gate
    ungroup(dot(normed, d_y, 1, 0), weights)
    grad_h = dot(w_own, d_y, 1, 1) * scale
    d_mixed = norm_back(grad_h, h_out, inv_out, 0)
    for k in range(COLS):
        for h in range(2):
            rows[pl.ds(h * COLS + k, NLANE, stride=2 * COLS), :] = to_message(d_mixed, k, h, ROWS)
    sums = jnp.concatenate([dot(flat_in, d_gate, 0, 0), weights[...]], axis=0)
    both = jnp.concatenate(
        [rows[...].reshape(NLANE, 2 * COLS, WIDTH), sums.reshape(NLANE, 2 * COLS, WIDTH)], axis=1
    )
    send[...] = both.reshape(2 * PAIRS, WIDTH).astype(BF16)


def grad_kernel(a_all, b_all, recv_d, d_a_own, d_a_near, d_b):
    d_mixed = split_rows(recv_d[...], 4)[:2]
    a_val = [a_all[y * WIDTH : (y + 1) * WIDTH] for y in range(2)]
    block = lane_block((HALF, WIDTH))
    totals = [None, None]
    for r in range(NROW):
        tiles = []
        for h in range(2):
            part = d_mixed[h][r * HALF : (r + 1) * HALF]
            nothing = jnp.zeros_like(part)
            tiles.append(
                jnp.concatenate(
                    [
                        jnp.where(block == cc % QUAD, part, nothing) if cc // QUAD == h else nothing
                        for cc in range(GROUP)
                    ],
                    axis=0,
                )
            )
        spread = jnp.concatenate(tiles, axis=1).astype(BF16)
        for y in range(2):
            side = 2 * r + y
            term = dot(b_all[side * WIDTH : (side + 1) * WIDTH], spread, 1, 0)
            totals[y] = term if totals[y] is None else totals[y] + term
            d_b[side * WIDTH : (side + 1) * WIDTH] = dot(a_val[y], spread, 1, 1).astype(BF16)
    is_first = lax.axis_index("y") == 0
    for h in range(2):
        first, second = (total[:, h * WIDTH : (h + 1) * WIDTH] for total in totals)
        d_a_own[h * WIDTH : (h + 1) * WIDTH] = jnp.where(is_first, first, second)
        d_a_near[h * WIDTH : (h + 1) * WIDTH] = jnp.where(is_first, second, first).astype(BF16)


def in_gather_order(values, lane):
    for bit in range(4):
        size = COLS << bit
        pairs = values.reshape(WIDTH // (2 * size), 2, size, WIDTH)
        swapped = jnp.concatenate([pairs[:, 1:], pairs[:, :1]], axis=1)
        values = jnp.where((lane >> bit) & 1 == 1, swapped, pairs).reshape(WIDTH, WIDTH)
    places = [0]
    for axis, step in GATHER:
        places += [place ^ (2 * step if axis == "z" else step) for place in places]
    return jnp.concatenate([values[p * COLS : (p + 1) * COLS] for p in places], axis=0)


def weight_kernel(
    wide_0, wide_1, w_ab, d_a_own, d_a_near, d_b, recv_d, d_a_sum, d_b_sum, send, proj, d_proj
):
    lane = lax.axis_index("z") * 2 + lax.axis_index("core")
    d_a = d_a_own[...] + d_a_near[...].astype(F32)
    d_a_sum[...] = d_a
    totals = []
    for y in range(2):
        total = d_b[y * WIDTH : (y + 1) * WIDTH].astype(F32)
        for r in range(1, NROW):
            side = 2 * r + y
            total = total + d_b[side * WIDTH : (side + 1) * WIDTH].astype(F32)
        totals.append(total)
    d_b_sum[...] = jnp.concatenate(totals, axis=0)
    tall = 4 * WIDTH
    tap = lax.broadcasted_iota(jnp.int32, (tall, TAPS), 1)
    source = tap // GROUP * WIDTH + lane * GROUP + tap % GROUP
    pick = (lax.broadcasted_iota(jnp.int32, (tall, TAPS), 0) == source).astype(F32)
    w_own = dot(pick.astype(BF16), w_ab[...], 0, 1)
    nothing = jnp.zeros_like(w_own)
    w_twice = jnp.concatenate(
        [jnp.concatenate([w_own, nothing], axis=1), jnp.concatenate([nothing, w_own], axis=1)],
        axis=0,
    ).astype(BF16)
    parts = []
    for i in range(0, ROWS, 2):
        lanes = slice(i * WIDTH, (i + 2) * WIDTH)
        part = jnp.concatenate([wide_0[:, lanes], wide_1[:, lanes]], axis=0)
        parts.append(part)
        values = dot(w_twice, part, 1, 1)
        for odd in range(2):
            proj[pl.ds(i + odd, TAPS, stride=ROWS), :] = values[odd * TAPS : (odd + 1) * TAPS]
    turned_a = jnp.concatenate(
        [in_gather_order(d_a[h * WIDTH : (h + 1) * WIDTH], lane).T for h in range(2)], axis=0
    )
    sides = [in_gather_order(total, lane).T for total in totals]
    turned_b = jnp.concatenate(
        [side[cc * HALF : (cc + 1) * HALF] for cc in range(GROUP) for side in sides], axis=0
    )
    for half, d_val in enumerate((turned_a, turned_b)):
        start = half * 2 * RES
        sig = jax.nn.sigmoid(proj[start : start + RES])
        value = proj[start + RES : start + 2 * RES]
        d_value = d_val * sig
        d_proj[start : start + RES] = d_value * value * (1.0 - sig)
        d_proj[start + RES : start + 2 * RES] = d_value
    sums = None
    for i in range(0, ROWS, 2):
        left = jnp.concatenate(
            [d_proj[pl.ds(i + odd, TAPS, stride=ROWS), :] for odd in range(2)], axis=0
        ).astype(BF16)
        both = dot(left, parts[i // 2], 1, 0)
        term = both[:TAPS, :WIDTH] + both[TAPS:, WIDTH:]
        sums = term if sums is None else sums + term
    others = recv_d[...].astype(F32).reshape(NLANE, 4 * COLS, WIDTH)[:, 2 * COLS :]
    own = jnp.concatenate([sums, jnp.sum(others, axis=0)], axis=0) * (1.0 / RES)
    for side in range(NSIDE):
        send[side * SHARE : (side + 1) * SHARE] = own.astype(BF16)


def join_kernel(d_a, d_b, sums, send):
    total = jnp.sum(sums[...].astype(F32).reshape(NSIDE, SHARE, WIDTH), axis=0)
    pieces = [
        half[part * WIDTH : (part + 1) * WIDTH].reshape(NLANE, COLS, WIDTH)
        for half in (d_a, d_b)
        for part in range(2)
    ]
    pieces.append(jnp.broadcast_to(total[None], (NLANE, SHARE, WIDTH)))
    send[...] = jnp.concatenate(pieces, axis=1).reshape(NLANE * FINAL, WIDTH).astype(BF16)


def last_kernel(
    recv, pair, mask, gain, w_ab, w_gate, normed_in, d_gate,
    grad_pair, grad_ab, grad_gate, grad_out, rows, weights, message,
):
    values = load_pairs(pair, rows)
    h_in, inv_in = layer_norm(values, 1)
    flat_in = normed_in[...]
    weights[...] = w_ab[...].astype(F32).T
    w_own = regroup(weights, 4).astype(BF16)
    proj = dot(w_own, flat_in, 1, 1)
    flags, *half_flags = mask_rows(mask)
    message[...] = recv[...].astype(F32)
    grads = []
    for half, size in enumerate((ROWS, HALF)):
        pieces = [
            [
                message[pl.ds((half * 2 + part) * COLS + k, NLANE, stride=FINAL), :]
                * (half_flags[part] if half else flags)[k : k + 1]
                for part in range(2)
            ]
            for k in range(COLS)
        ]
        d_val = from_message(pieces, size)
        sig = jax.nn.sigmoid(proj[half * 256 : half * 256 + 128])
        value = proj[half * 256 + 128 : half * 256 + 256]
        d_value = d_val * sig
        grads += [d_value * value * (1.0 - sig), d_value]
    d_proj = jnp.concatenate(grads, axis=0).astype(BF16)
    d_in = dot(d_proj, w_own, 0, 0) + dot(d_gate[...], w_gate[...], 1, 1)
    store_pairs(norm_back(d_in * gain[...], h_in, inv_in, 1), rows, grad_pair)
    for blk in range(4):
        for cc in range(GROUP):
            weights[pl.ds(blk * WIDTH + cc, NLANE, stride=GROUP), :] = message[
                pl.ds(4 * COLS + blk * GROUP + cc, NLANE, stride=FINAL), :
            ]
    grad_ab[...] = weights[...].T
    others = message[...].reshape(NLANE, FINAL, WIDTH)[:, 4 * COLS + TAPS :].reshape(PAIRS, WIDTH)
    grad_gate[...] = others[:WIDTH]
    grad_out[...] = others[WIDTH:]


def call(kernel, outs, scratch, *args, places=None):
    return pl.pallas_call(
        kernel,
        out_shape=[jax.ShapeDtypeStruct(shape, dtype) for shape, dtype in outs],
        in_specs=[
            pl.BlockSpec(memory_space=pltpu.VMEM if places is None else places[n])
            for n in range(len(args))
        ],
        scratch_shapes=scratch,
        compiler_params=pltpu.CompilerParams(vmem_limit_bytes=32 * 1024 * 1024),
    )(*args)


LANES = ("z", "core")
SIDES = ("row", "y")


def exchange(values, axes):
    return lax.all_to_all(values, axes, 0, 0, tiled=True)


def swap(values, axis, step):
    return lax.ppermute(values, axis, [(n, n ^ step) for n in range(lax.axis_size(axis))])


def beside(values, axes, *swaps):
    values, *held = lax.optimization_barrier((values, *(array for array, _, _ in swaps)))
    came = [swap(array, axis, step) for array, (_, axis, step) in zip(held, swaps)]
    return lax.optimization_barrier((exchange(values, axes), held, came))


def on_device(pair, pair_mask, ln_in_gain, w_ab, w_gate, ln_out_gain, w_out, cotangent):
    pair_mask = pair_mask.T
    gain_in = ln_in_gain.reshape(1, WIDTH)
    gain_out = ln_out_gain.reshape(1, WIDTH)
    flat = (PAIRS, WIDTH)
    twice = (2 * PAIRS, WIDTH)
    copies = (NSIDE * WIDTH, WIDTH)
    blocks = (ROWS, COLS, WIDTH)
    square = (WIDTH, WIDTH)
    wide = (WIDTH, 4 * WIDTH)
    tall = (4 * WIDTH, WIDTH)
    last = (NLANE * FINAL, WIDTH)
    inputs = (pair, pair_mask, gain_in, w_ab, gain_out, w_gate, w_out, cotangent)
    *inputs, normed_in, wide_in, send_ab = call(
        project_kernel,
        [(array.shape, array.dtype) for array in inputs]
        + [(flat, BF16), ((COLS, ROWS * WIDTH), BF16), (twice, BF16)],
        [
            pltpu.VMEM(flat, F32),
            pltpu.VMEM(tall, F32),
            pltpu.VMEM(twice, F32),
            pltpu.SemaphoreType.DMA((len(inputs),)),
        ],
        *(pltpu.with_memory_space_constraint(array, pltpu.HBM) for array in inputs),
        places=[pltpu.HBM] * len(inputs),
    )
    pair, pair_mask, gain_in, w_ab, gain_out, w_gate, w_out, cotangent = inputs
    recv_ab, held, came = beside(send_ab, LANES)
    held = wide_in
    (send_b,) = call(spread_kernel, [(copies, BF16)], [], recv_ab)
    b_all, (held, _), (came, recv_near) = beside(
        send_b, SIDES, (held, *GATHER[0]), (recv_ab, "y", 1)
    )
    held = jnp.concatenate([held, came], axis=0)
    send_mixed, a_all = call(
        mix_kernel, [(flat, BF16), ((2 * WIDTH, 2 * WIDTH), BF16)], [], recv_ab, recv_near, b_all
    )
    recv_mixed, held, came = beside(send_mixed, LANES, (held, *GATHER[1]))
    held = jnp.concatenate(held + came, axis=0)
    update, send_d, d_gate = call(
        middle_kernel,
        [(blocks, BF16), (twice, BF16), (flat, BF16)],
        [pltpu.VMEM(flat, F32), pltpu.VMEM(square, F32)],
        recv_mixed, normed_in, cotangent, w_gate, gain_out, w_out,
    )
    recv_d, held, came = beside(send_d, LANES, (held, *GATHER[2]))
    held = jnp.concatenate(held + came, axis=0)
    d_a_own, d_a_near, d_b = call(
        grad_kernel, [(flat, F32), (flat, BF16), (copies, BF16)], [], a_all, b_all, recv_d
    )
    d_b, (_, held), (d_a_near, came) = beside(d_b, SIDES, (d_a_near, "y", 1), (held, *GATHER[3]))
    wide_parts = [held, came]
    d_a, d_b, sums = call(
        weight_kernel,
        [(flat, F32), (flat, F32), ((NSIDE * SHARE, WIDTH), BF16)],
        [pltpu.VMEM((TAPS * ROWS, WIDTH), F32), pltpu.VMEM((TAPS * ROWS, WIDTH), F32)],
        *wide_parts, w_ab, d_a_own, d_a_near, d_b, recv_d,
    )
    sums = exchange(sums, SIDES)
    (send_last,) = call(join_kernel, [(last, BF16)], [], d_a, d_b, sums)
    recv_last = exchange(send_last, LANES)
    grad_pair, grad_ab, grad_gate, grad_out = call(
        last_kernel,
        [(blocks, BF16), (wide, F32), (square, F32), (square, F32)],
        [pltpu.VMEM(flat, F32), pltpu.VMEM(tall, F32), pltpu.VMEM(last, F32)],
        recv_last, pair, pair_mask, gain_in, w_ab, w_gate, normed_in, d_gate,
    )
    return update, grad_pair, grad_ab, grad_gate, grad_out


def solution(mesh):
    split = Mesh(mesh.devices.reshape(NROW, 8, 2, 2), ("row", "z", "y", "core"))
    cols = ("z", "y", "core")
    blocks = P("row", cols, None)
    placed = (blocks, P("row", cols), P(), P(), P(), P(), P(), blocks)
    return jax.shard_map(
        on_device,
        mesh=split,
        in_specs=placed,
        out_specs=(blocks, blocks, P(), P(), P()),
        check_vma=False,
    )
```

time: 148 us -> 120 us (0.81)
  blocking collectives: 136 us -> 74.8 us
  waiting for transfers between devices: 0 us -> 18.4 us
  starting transfers between devices: 0 us -> 16.4 us
  local copies, waits for them, and re-layouts: 5.63 us -> 0 us
  Pallas kernels: 4.44 us -> 9.52 us
    all_to_all x8 -> x5, blocking collectives: 136 us -> 74.8 us  [exchange(): return lax.all_to_all(values, axes, 0, 0, tiled=True)]
    all_to_all x0 -> x2, starting transfers between devices: none -> 12.7 us  [exchange(): return lax.all_to_all(values, axes, 0, 0, tiled=True)]
    ppermute x0 -> x6, waiting for transfers between devices: none -> 11.9 us  [swap(): lax.ppermute(values, axis, [(n, n ^ step) for n in range(lax.axis_size(ax...]
    all_to_all x0 -> x2, waiting for transfers between devices: none -> 6.51 us  [exchange(): return lax.all_to_all(values, axes, 0, 0, tiled=True)]
    pallas_call x6 -> x8, Pallas kernels: 4.44 us -> 9.52 us  [call(): pl.pallas_call(kernel, out_shape=[jax.ShapeDtypeStruct(shape, dtype) for...]
    unnamed x20 -> x0, local copies, waits for them, and re-layouts: 4.67 us -> none
    ppermute x0 -> x6, starting transfers between devices: none -> 3.67 us  [swap(): lax.ppermute(values, axis, [(n, n ^ step) for n in range(lax.axis_size(ax...]
  transfers between devices with their start and end apart: 0 -> 8, of which waited for: 0 -> 5; matrix products, arithmetic and copies ran while one was open for 0% -> 0% of each run, Pallas kernels for 0% -> 0%
where the time goes in v3:
time: 120 us
  blocking collectives  74.8 us (62%)
  waiting for transfers between devices  18.4 us (15%)
  starting transfers between devices  16.4 us (14%)
  Pallas kernels  9.52 us (8%)
    all_to_all x5, blocking collectives, exchange(): return lax.all_to_all(values, axes, 0, 0, tiled=True)  74.8 us
    all_to_all x2, starting transfers between devices, exchange(): return lax.all_to_all(values, axes, 0, 0, tiled=True)  12.7 us
    ppermute x6, waiting for transfers between devices, swap(): lax.ppermute(values, axis, [(n, n ^ step) for n in range(lax.axis_size(ax...  11.9 us
    pallas_call x8, Pallas kernels, call(): pl.pallas_call(kernel, out_shape=[jax.ShapeDtypeStruct(shape, dtype) for...  9.52 us
    all_to_all x2, waiting for transfers between devices, exchange(): return lax.all_to_all(values, axes, 0, 0, tiled=True)  6.51 us
    ppermute x6, starting transfers between devices, swap(): lax.ppermute(values, axis, [(n, n ^ step) for n in range(lax.axis_size(ax...  3.67 us
  transfers between devices with their start and end apart: 8, of which 5 were waited for; matrix products, arithmetic and copies ran while one was open for 0% of the time, Pallas kernels for 0%

profile of v3, /device:TPU:1, one launch (start us, length us, event | category | flops | bytes accessed | tf_op | source)
XLA Modules:
  0.0 119.9 jit_solution(5054247447670032376)
XLA Ops:
  0.6 2.1 %shard_map.119 = (bf16[32,8,128]{2,1,0:T(8,128)(2,1)S(1)}, s32[8,32]{1,0:T(8,128)S(1)}, f32[1,128]{1,0:T(1,128)S(1)}, bf16[128,512]{1,0:T(8,128)(2,1)S(1)}, f32[...) custom-call(bf16[32,8,128]{2,1,0:T(8,128)(2,1)} %refs_0_.1, ...), custom_call_target="tpu_custom_call" | custom-call | tf_op jit(solution)/shard_map/pallas_call | solution.py:407
  2.8 18.9 %all_to_all.82 = bf16[16,32,128]{2,1,0:T(8,128)(2,1)S(1)} all-to-all(bf16[16,32,128]{2,1,0:T(8,128)(2,1)S(1)} %bitcast.30), channel_id=1, replica_groups=mesh['row'=8,'z'=8,'y'=2,'core'=2] {'z','core'}, dimensions={0} | all-to-all | bytes 262144 | tf_op jit(solution)/shard_map/all_to_all | solution.py:424
  21.7 0.9 shard_map.120
  22.6 6.8 %all-to-all-start.1 = ((bf16[16,128,128]{2,1,0:T(8,128)(2,1)}), bf16[16,128,128]{2,1,0:T(8,128)(2,1)S(1)}, u32[]{:S(2)}, u32[]{:S(2)}) async-start(bf16[16,128,128]{2,1,0:T(8,128)(2,1)} %bitcast.5), calls=%async_computation.1 | async-start | bytes 1048576 | tf_op jit(solution)/shard_map/all_to_all | solution.py:424
  29.3 1.4 %collective-permute-start.1 = (bf16[512,128]{1,0:T(8,128)(2,1)S(1)}, bf16[512,128]{1,0:T(8,128)(2,1)S(1)}, u32[]{:S(2)}, u32[]{:S(2)}) collective-permute-start(bf16[512,128]{1,0:T(8,128)(2,1)S(1)} %bitcast.25), channel_id=1, source_target_pairs={{0,2},{2,0},{1,3},{3,1},{4,6},{6,4},{5,7},{7,5},{8,10},{10,8},{9,1... | collective-permute-start | bytes 393224 | tf_op jit(solution)/shard_map/ppermute | solution.py:428
  30.7 0.6 collective-permute-start
  31.3 7.5 %collective-permute-done = bf16[8,4096]{1,0:T(8,128)(2,1)S(1)} collective-permute-done((bf16[8,4096]{1,0:T(8,128)(2,1)S(1)}, bf16[8,4096]{1,0:T(8,128)(2,1)S(1)}, u32[]{:S(2)}, u32[]{:S(2)}) %collective-permute-start) | collective-permute-done | bytes 65568 | tf_op jit(solution)/shard_map/ppermute | solution.py:428
  38.9 1.4 %collective-permute-done.1.recv_near = bf16[512,128]{1,0:T(8,128)(2,1)S(1)} collective-permute-done((bf16[512,128]{1,0:T(8,128)(2,1)S(1)}, bf16[512,128]{1,0:T(8,128)(2,1)S(1)}, u32[]{:S(2)}, u32[]{:S(2)}) %collective-permute-start.1) | collective-permute-done | bytes 131104 | tf_op jit(solution)/shard_map/ppermute | solution.py:428
  40.2 0.5 all-to-all-done.1
  40.8 0.5 shard_map.121
  41.3 0.1 collective-permute-start.2
  41.4 12.8 %all_to_all.83 = bf16[16,16,128]{2,1,0:T(8,128)(2,1)S(1)} all-to-all(bf16[16,16,128]{2,1,0:T(8,128)(2,1)S(1)} %bitcast.32), channel_id=1, replica_groups=mesh['row'=8,'z'=8,'y'=2,'core'=2] {'z','core'}, dimensions={0} | all-to-all | bytes 131072 | tf_op jit(solution)/shard_map/all_to_all | solution.py:424
  54.2 0.0 collective-permute-done.2
  54.2 1.1 shard_map.122
  55.4 0.2 collective-permute-start.3
  55.6 12.8 %all_to_all.84 = bf16[16,32,128]{2,1,0:T(8,128)(2,1)S(1)} all-to-all(bf16[16,32,128]{2,1,0:T(8,128)(2,1)S(1)} %bitcast.31), channel_id=1, replica_groups=mesh['row'=8,'z'=8,'y'=2,'core'=2] {'z','core'}, dimensions={0} | all-to-all | bytes 262144 | tf_op jit(solution)/shard_map/all_to_all | solution.py:424
  68.4 0.0 collective-permute-done.3
  68.4 1.5 %shard_map.123 = (f32[256,128]{1,0:T(8,128)S(1)}, bf16[256,128]{1,0:T(8,128)(2,1)S(1)}, bf16[2048,128]{1,0:T(8,128)(2,1)}) custom-call(bf16[256,256]{1,0:T(8,128)(2,1)S(1)} %get-tuple-element.74.a_all, bf16[2048,128]{1,0:T(8,128)(2,1)S(1)} %bitcast.18, bf16[512,128]{1,0:T(8,128)(2,1)S(1)} %bitcast.22), custom_call_target="tpu_custom_call" | custom-call | tf_op jit(solution)/shard_map/pallas_call | solution.py:407
  69.9 0.0 collective-permute-start.5
  69.9 6.0 %all-to-all-start.4 = ((bf16[16,128,128]{2,1,0:T(8,128)(2,1)}), bf16[16,128,128]{2,1,0:T(8,128)(2,1)S(1)}, u32[]{:S(2)}, u32[]{:S(2)}) async-start(bf16[16,128,128]{2,1,0:T(8,128)(2,1)} %bitcast.11), calls=%async_computation.4 | async-start | bytes 1048576 | tf_op jit(solution)/shard_map/all_to_all | solution.py:424
  75.9 1.4 %collective-permute-start.4 = (bf16[256,128]{1,0:T(8,128)(2,1)S(1)}, bf16[256,128]{1,0:T(8,128)(2,1)S(1)}, u32[]{:S(2)}, u32[]{:S(2)}) collective-permute-start(bf16[256,128]{1,0:T(8,128)(2,1)S(1)} %get-tuple-element.86), channel_id=1, source_target_pairs={{0,2},{2,0},{1,3},{3,1},{4,6},{6,4},{5,7},{7,5},{8,10},{10,8},{9,1... | collective-permute-start | bytes 196616 | tf_op jit(solution)/shard_map/ppermute | solution.py:428
  77.3 3.0 %collective-permute-done.4.d_a_near = bf16[256,128]{1,0:T(8,128)(2,1)S(1)} collective-permute-done((bf16[256,128]{1,0:T(8,128)(2,1)S(1)}, bf16[256,128]{1,0:T(8,128)(2,1)S(1)}, u32[]{:S(2)}, u32[]{:S(2)}) %collective-permute-start.4) | collective-permute-done | bytes 65568 | tf_op jit(solution)/shard_map/ppermute | solution.py:428
  80.3 6.0 %all-to-all-done.4 = bf16[16,128,128]{2,1,0:T(8,128)(2,1)S(1)} async-done(((bf16[16,128,128]{2,1,0:T(8,128)(2,1)}), bf16[16,128,128]{2,1,0:T(8,128)(2,1)S(1)}, u32[]{:S(2)}, u32[]{:S(2)}) %all-to-all-start.4) | async-done | bytes 524320 | tf_op jit(solution)/shard_map/all_to_all | solution.py:424
  86.2 0.0 collective-permute-done.5.wide_1
  86.2 1.3 %shard_map.124 = (f32[256,128]{1,0:T(8,128)S(1)}, f32[256,128]{1,0:T(8,128)S(1)}, bf16[768,128]{1,0:T(8,128)(2,1)S(1)}) custom-call(bf16[64,4096]{1,0:T(8,128)(2,1)S(1)} %pad_maximum_fusion.wide_0, bf16[64,4096]{1,0:T(8,128)(2,1)S(1)} %collective-permute-done.5.wide_1, bf16[128,512]{1,0:T(8,128)(2,1)S(1)} %get-tuple-element.90.w_ab, ...), custom_call_target="tpu_custom_call" | custom-call | tf_op jit(solution)/shard_map/pallas_call | solution.py:407
  87.6 11.5 %all_to_all.85 = bf16[16,48,128]{2,1,0:T(8,128)(2,1)S(1)} all-to-all(bf16[16,48,128]{2,1,0:T(8,128)(2,1)S(1)} %bitcast.29), channel_id=1, replica_groups=mesh['row'=8,'z'=8,'y'=2,'core'=2] {'row','y'}, dimensions={0} | all-to-all | bytes 393216 | tf_op jit(solution)/shard_map/all_to_all | solution.py:424
  99.1 18.7 %all_to_all.86 = bf16[16,80,128]{2,1,0:T(8,128)(2,1)S(1)} all-to-all(bf16[16,80,128]{2,1,0:T(8,128)(2,1)S(1)} %bitcast.21), channel_id=1, replica_groups=mesh['row'=8,'z'=8,'y'=2,'core'=2] {'z','core'}, dimensions={0} | all-to-all | bytes 655360 | tf_op jit(solution)/shard_map/all_to_all | solution.py:424
  117.8 2.1 %shard_map.126 = (bf16[32,8,128]{2,1,0:T(8,128)(2,1)}, f32[128,512]{1,0:T(8,128)}, f32[128,128]{1,0:T(8,128)}, f32[128,128]{1,0:T(8,128)}) custom-call(bf16[1280,128]{1,0:T(8,128)(2,1)S(1)} %bitcast.20, bf16[32,8,128]{2,1,0:T(8,128)(2,1)S(1)} %get-tuple-element.97.pair, s32[8,32]{1,0:T(8,128)S(1)} %get-tuple-element.98.mask, ...), custom_call_target="tpu_custom_call" | custom-call | tf_op jit(solution)/shard_map/pallas_call | solution.py:407
  (4 shorter events, 0.1 us)
Async XLA Ops:
  22.6 18.2 %all-to-all-start.1 = ((bf16[16,128,128]{2,1,0:T(8,128)(2,1)}), bf16[16,128,128]{2,1,0:T(8,128)(2,1)S(1)}, u32[]{:S(2)}, u32[]{:S(2)}) async-start(bf16[16,128,128]{2,1,0:T(8,128)(2,1)} %bitcast.5), calls=%async_computation.1 | async-start | bytes 1048576 | tf_op jit(solution)/shard_map/all_to_all | solution.py:424
  29.3 10.9 %collective-permute-start.1 = (bf16[512,128]{1,0:T(8,128)(2,1)S(1)}, bf16[512,128]{1,0:T(8,128)(2,1)S(1)}, u32[]{:S(2)}, u32[]{:S(2)}) collective-permute-start(bf16[512,128]{1,0:T(8,128)(2,1)S(1)} %bitcast.25), channel_id=1, source_target_pairs={{0,2},{2,0},{1,3},{3,1},{4,6},{6,4},{5,7},{7,5},{8,10},{10,8},{9,1... | collective-permute-start | bytes 393224 | tf_op jit(solution)/shard_map/ppermute | solution.py:428
  30.7 8.2 %collective-permute-start = (bf16[8,4096]{1,0:T(8,128)(2,1)S(1)}, bf16[8,4096]{1,0:T(8,128)(2,1)S(1)}, u32[]{:S(2)}, u32[]{:S(2)}) collective-permute-start(bf16[8,4096]{1,0:T(8,128)(2,1)S(1)} %get-tuple-element.63), channel_id=1, source_target_pairs={{0,16},{4,20},{8,24},{12,28},{16,0},{20,4},{24,8},{28,12},{1,17},{... | collective-permute-start | bytes 196616 | tf_op jit(solution)/shard_map/ppermute | solution.py:428
  41.3 12.9 %collective-permute-start.2 = (bf16[16,4096]{1,0:T(8,128)(2,1)S(1)}, bf16[16,4096]{1,0:T(8,128)(2,1)S(1)}, u32[]{:S(2)}, u32[]{:S(2)}) collective-permute-start(bf16[16,4096]{1,0:T(8,128)(2,1)S(1)} %pad_maximum_fusion.2), channel_id=1, source_target_pairs={{0,8},{4,12},{8,0},{12,4},{16,24},{20,28},{24,16},{28,20},{1,9},{5... | collective-permute-start | bytes 393224 | tf_op jit(solution)/shard_map/ppermute | solution.py:428
  55.4 13.0 %collective-permute-start.3 = (bf16[32,4096]{1,0:T(8,128)(2,1)S(1)}, bf16[32,4096]{1,0:T(8,128)(2,1)S(1)}, u32[]{:S(2)}, u32[]{:S(2)}) collective-permute-start(bf16[32,4096]{1,0:T(8,128)(2,1)S(1)} %pad_maximum_fusion.1), channel_id=1, source_target_pairs={{0,4},{4,0},{8,12},{12,8},{16,20},{20,16},{24,28},{28,24},{1,5},{5... | collective-permute-start | bytes 786440 | tf_op jit(solution)/shard_map/ppermute | solution.py:428
  69.9 16.3 %collective-permute-start.5 = (bf16[64,4096]{1,0:T(8,128)(2,1)S(1)}, bf16[64,4096]{1,0:T(8,128)(2,1)S(1)}, u32[]{:S(2)}, u32[]{:S(2)}) collective-permute-start(bf16[64,4096]{1,0:T(8,128)(2,1)S(1)} %pad_maximum_fusion.wide_0), channel_id=1, source_target_pairs={{0,1},{1,0},{2,3},{3,2},{4,5},{5,4},{6,7},{7,6},{8,9},{9,8},{10,11... | collective-permute-start | bytes 1572872 | tf_op jit(solution)/shard_map/ppermute | solution.py:428
  69.9 16.3 %all-to-all-start.4 = ((bf16[16,128,128]{2,1,0:T(8,128)(2,1)}), bf16[16,128,128]{2,1,0:T(8,128)(2,1)S(1)}, u32[]{:S(2)}, u32[]{:S(2)}) async-start(bf16[16,128,128]{2,1,0:T(8,128)(2,1)} %bitcast.11), calls=%async_computation.4 | async-start | bytes 1048576 | tf_op jit(solution)/shard_map/all_to_all | solution.py:424
  75.9 4.3 %collective-permute-start.4 = (bf16[256,128]{1,0:T(8,128)(2,1)S(1)}, bf16[256,128]{1,0:T(8,128)(2,1)S(1)}, u32[]{:S(2)}, u32[]{:S(2)}) collective-permute-start(bf16[256,128]{1,0:T(8,128)(2,1)S(1)} %get-tuple-element.86), channel_id=1, source_target_pairs={{0,2},{2,0},{1,3},{3,1},{4,6},{6,4},{5,7},{7,5},{8,10},{10,8},{9,1... | collective-permute-start | bytes 196616 | tf_op jit(solution)/shard_map/ppermute | solution.py:428

commit v4 on v3

--- a/solution.py
+++ b/solution.py
@@ -17,7 +17,7 @@
 RES = 256
 TAPS = 4 * GROUP
 SHARE = TAPS + 2 * WIDTH // NLANE
-FINAL = 4 * COLS + SHARE
+FINAL = 4 * COLS + SHARE // 2
 GATHER = (("z", 4), ("z", 2), ("z", 1), ("core", 1))
 
 
@@ -172,22 +172,17 @@
     send[...] = message[...].astype(BF16)
 
 
-def spread_kernel(recv, send):
+def spread_kernel(recv, send, a_own):
     parts = split_rows(recv[...], 4)
+    a_own[...] = jnp.concatenate(parts[:2], axis=1).astype(BF16)
     for side in range(NSIDE):
         send[side * WIDTH : (side + 1) * WIDTH] = parts[2 + side % 2].astype(BF16)
 
 
-def mix_kernel(recv, recv_near, b_all, send, a_all):
-    own, near = split_rows(recv[...], 4), split_rows(recv_near[...], 4)
+def mix_kernel(own, near, b_all, send, a_all):
     is_first = lax.axis_index("y") == 0
-    a_val = []
-    for first, second in ((own, near), (near, own)):
-        a_val.append(
-            jnp.concatenate(
-                [jnp.where(is_first, first[h], second[h]) for h in range(2)], axis=1
-            ).astype(BF16)
-        )
+    own, near = own[...], near[...]
+    a_val = [jnp.where(is_first, own, near), jnp.where(is_first, near, own)]
     a_all[...] = jnp.concatenate(a_val, axis=0)
     block = lane_block((HALF, WIDTH))
     pieces = []
@@ -209,8 +204,31 @@
     send[...] = jnp.concatenate(pieces, axis=0).astype(BF16)
 
 
+def prepare_kernel(
+    pair, w_ab, normed_in, cotangent, w_gate, gain_out, w_out,
+    h_in, inv_in, w_ab_own, factors, gate, cot, scale, w_out_own, rows, weights,
+):
+    h_in[...], inv_in[...] = layer_norm(load_pairs(pair, rows), 1)
+    flat_in = normed_in[...]
+    weights[...] = w_out[...].astype(F32)
+    w_out_own[...] = regroup(weights, 1).astype(BF16)
+    scale[...] = column_of(gain_out[...])
+    gate[...] = jax.nn.sigmoid(dot(flat_in, w_gate[...], 1, 0))
+    cot[...] = load_pairs(cotangent, rows)
+    for blk in range(4):
+        weights[...] = w_ab[:, blk * WIDTH : (blk + 1) * WIDTH].astype(F32).T
+        w_ab_own[blk * WIDTH : (blk + 1) * WIDTH] = regroup(weights, 1).astype(BF16)
+    proj = dot(w_ab_own[...], flat_in, 1, 1)
+    for half in range(2):
+        start = half * 2 * WIDTH
+        sig = jax.nn.sigmoid(proj[start : start + WIDTH])
+        value = proj[start + WIDTH : start + 2 * WIDTH]
+        factors[start : start + WIDTH] = value * sig * (1.0 - sig)
+        factors[start + WIDTH : start + 2 * WIDTH] = sig
+
+
 def middle_kernel(
-    recv, normed_in, cotangent, w_gate, gain, w_out,
+    recv, normed_in, gate, cot, scale, w_out_own,
     update, send, d_gate_out, rows, weights,
 ):
     rows[...] = recv[...].astype(F32)
@@ -222,15 +240,13 @@
         ROWS,
     )
     h_out, inv_out = layer_norm(mixed, 0)
-    scale = column_of(gain[...])
+    scale = scale[...]
     normed = (h_out * scale).astype(BF16)
-    weights[...] = w_out[...].astype(F32)
-    w_own = regroup(weights, 1).astype(BF16)
+    w_own = w_out_own[...]
     y_val = dot(normed, w_own, 0, 0)
     flat_in = normed_in[...]
-    gate = jax.nn.sigmoid(dot(flat_in, w_gate[...], 1, 0))
+    gate, cot = gate[...], cot[...]
     store_pairs(gate * y_val, rows, update)
-    cot = load_pairs(cotangent, rows)
     d_y = (cot * gate).astype(BF16)
     d_gate = (cot * y_val * gate * (1.0 - gate)).astype(BF16)
     d_gate_out[...] = d_gate
@@ -358,20 +374,18 @@
         for half in (d_a, d_b)
         for part in range(2)
     ]
-    pieces.append(jnp.broadcast_to(total[None], (NLANE, SHARE, WIDTH)))
+    shares = jnp.broadcast_to(
+        total.reshape(1, 2, SHARE // 2, WIDTH), (NLANE // 2, 2, SHARE // 2, WIDTH)
+    )
+    pieces.append(shares.reshape(NLANE, SHARE // 2, WIDTH))
     send[...] = jnp.concatenate(pieces, axis=1).reshape(NLANE * FINAL, WIDTH).astype(BF16)
 
 
 def last_kernel(
-    recv, pair, mask, gain, w_ab, w_gate, normed_in, d_gate,
-    grad_pair, grad_ab, grad_gate, grad_out, rows, weights, message,
+    recv, mask, gain, w_gate, d_gate, h_in, inv_in, w_ab_own, factors,
+    grad_pair, rows, message,
 ):
-    values = load_pairs(pair, rows)
-    h_in, inv_in = layer_norm(values, 1)
-    flat_in = normed_in[...]
-    weights[...] = w_ab[...].astype(F32).T
-    w_own = regroup(weights, 4).astype(BF16)
-    proj = dot(w_own, flat_in, 1, 1)
+    w_own = w_ab_own[...]
     flags, *half_flags = mask_rows(mask)
     message[...] = recv[...].astype(F32)
     grads = []
@@ -385,25 +399,37 @@
             for k in range(COLS)
         ]
         d_val = from_message(pieces, size)
-        sig = jax.nn.sigmoid(proj[half * 256 : half * 256 + 128])
-        value = proj[half * 256 + 128 : half * 256 + 256]
-        d_value = d_val * sig
-        grads += [d_value * value * (1.0 - sig), d_value]
+        start = half * 2 * WIDTH
+        grads += [
+            d_val * factors[start : start + WIDTH],
+            d_val * factors[start + WIDTH : start + 2 * WIDTH],
+        ]
     d_proj = jnp.concatenate(grads, axis=0).astype(BF16)
     d_in = dot(d_proj, w_own, 0, 0) + dot(d_gate[...], w_gate[...], 1, 1)
-    store_pairs(norm_back(d_in * gain[...], h_in, inv_in, 1), rows, grad_pair)
+    store_pairs(norm_back(d_in * gain[...], h_in[...], inv_in[...], 1), rows, grad_pair)
+
+
+def sums_kernel(recv, recv_near, grad_ab, grad_gate, grad_out, weights, message):
+    own, near = (
+        part[...].astype(F32).reshape(NLANE, FINAL, WIDTH)[:, 4 * COLS :]
+        for part in (recv, recv_near)
+    )
+    is_first = lax.axis_index("core") == 0
+    both = [jnp.where(is_first, own, near), jnp.where(is_first, near, own)]
+    both = jnp.concatenate(both, axis=1)
+    message[...] = both.reshape(NLANE * SHARE, WIDTH)
     for blk in range(4):
         for cc in range(GROUP):
             weights[pl.ds(blk * WIDTH + cc, NLANE, stride=GROUP), :] = message[
-                pl.ds(4 * COLS + blk * GROUP + cc, NLANE, stride=FINAL), :
+                pl.ds(blk * GROUP + cc, NLANE, stride=SHARE), :
             ]
     grad_ab[...] = weights[...].T
-    others = message[...].reshape(NLANE, FINAL, WIDTH)[:, 4 * COLS + TAPS :].reshape(PAIRS, WIDTH)
+    others = both[:, TAPS:].reshape(PAIRS, WIDTH)
     grad_gate[...] = others[:WIDTH]
     grad_out[...] = others[WIDTH:]
 
 
-def call(kernel, outs, scratch, *args, places=None):
+def call(kernel, outs, scratch, *args, places=None, cost=None):
     return pl.pallas_call(
         kernel,
         out_shape=[jax.ShapeDtypeStruct(shape, dtype) for shape, dtype in outs],
@@ -413,6 +439,7 @@
         ],
         scratch_shapes=scratch,
         compiler_params=pltpu.CompilerParams(vmem_limit_bytes=32 * 1024 * 1024),
+        cost_estimate=cost,
     )(*args)
 
 
@@ -429,7 +456,7 @@
 
 
 def beside(values, axes, *swaps):
-    values, *held = lax.optimization_barrier((values, *(array for array, _, _ in swaps)))
+    held = [array for array, _, _ in swaps]
     came = [swap(array, axis, step) for array, (_, axis, step) in zip(held, swaps)]
     return lax.optimization_barrier((exchange(values, axes), held, came))
 
@@ -462,14 +489,27 @@
     )
     pair, pair_mask, gain_in, w_ab, gain_out, w_gate, w_out, cotangent = inputs
     recv_ab, held, came = beside(send_ab, LANES)
-    held = wide_in
-    (send_b,) = call(spread_kernel, [(copies, BF16)], [], recv_ab)
-    b_all, (held, _), (came, recv_near) = beside(
-        send_b, SIDES, (held, *GATHER[0]), (recv_ab, "y", 1)
-    )
+    recv_ab, held = lax.optimization_barrier((recv_ab, wide_in))
+    send_b, a_own = call(spread_kernel, [(copies, BF16), ((WIDTH, 2 * WIDTH), BF16)], [], recv_ab)
+    send_b, held, a_own, normed_in = lax.optimization_barrier((send_b, held, a_own, normed_in))
+    prepared = call(
+        prepare_kernel,
+        [
+            (flat, F32), ((PAIRS, 1), F32), (tall, BF16), ((4 * WIDTH, PAIRS), F32),
+            (flat, F32), (flat, F32), ((WIDTH, 1), F32), (square, BF16),
+        ],
+        [pltpu.VMEM(flat, F32), pltpu.VMEM(square, F32)],
+        pair, w_ab, normed_in, cotangent, w_gate, gain_out, w_out,
+        cost=pl.CostEstimate(flops=150_000_000, bytes_accessed=3000000, transcendentals=200_000),
+    )
+    came, a_near = swap(held, *GATHER[0]), swap(a_own, "y", 1)
+    b_all, held, came, a_own, a_near, prepared = lax.optimization_barrier(
+        (exchange(send_b, SIDES), held, came, a_own, a_near, prepared)
+    )
+    h_in, inv_in, w_ab_own, factors, gate, cot, scale, w_out_own = prepared
     held = jnp.concatenate([held, came], axis=0)
     send_mixed, a_all = call(
-        mix_kernel, [(flat, BF16), ((2 * WIDTH, 2 * WIDTH), BF16)], [], recv_ab, recv_near, b_all
+        mix_kernel, [(flat, BF16), ((2 * WIDTH, 2 * WIDTH), BF16)], [], a_own, a_near, b_all
     )
     recv_mixed, held, came = beside(send_mixed, LANES, (held, *GATHER[1]))
     held = jnp.concatenate(held + came, axis=0)
@@ -477,7 +517,7 @@
         middle_kernel,
         [(blocks, BF16), (twice, BF16), (flat, BF16)],
         [pltpu.VMEM(flat, F32), pltpu.VMEM(square, F32)],
-        recv_mixed, normed_in, cotangent, w_gate, gain_out, w_out,
+        recv_mixed, normed_in, gate, cot, scale, w_out_own,
     )
     recv_d, held, came = beside(send_d, LANES, (held, *GATHER[2]))
     held = jnp.concatenate(held + came, axis=0)
@@ -495,11 +535,19 @@
     sums = exchange(sums, SIDES)
     (send_last,) = call(join_kernel, [(last, BF16)], [], d_a, d_b, sums)
     recv_last = exchange(send_last, LANES)
-    grad_pair, grad_ab, grad_gate, grad_out = call(
+    recv_near = swap(recv_last, "core", 1)
+    (grad_pair,) = call(
         last_kernel,
-        [(blocks, BF16), (wide, F32), (square, F32), (square, F32)],
-        [pltpu.VMEM(flat, F32), pltpu.VMEM(tall, F32), pltpu.VMEM(last, F32)],
-        recv_last, pair, pair_mask, gain_in, w_ab, w_gate, normed_in, d_gate,
+        [(blocks, BF16)],
+        [pltpu.VMEM(flat, F32), pltpu.VMEM(last, F32)],
+        recv_last, pair_mask, gain_in, w_gate, d_gate, h_in, inv_in, w_ab_own, factors,
+    )
+    recv_near, grad_pair = lax.optimization_barrier((recv_near, grad_pair))
+    grad_ab, grad_gate, grad_out = call(
+        sums_kernel,
+        [(wide, F32), (square, F32), (square, F32)],
+        [pltpu.VMEM(tall, F32), pltpu.VMEM((NLANE * SHARE, WIDTH), F32)],
+        recv_last, recv_near,
     )
     return update, grad_pair, grad_ab, grad_gate, grad_out
 

time: 120 us -> 117 us (0.975)
  blocking collectives: 74.8 us -> 72.3 us
  starting transfers between devices: 16.4 us -> 15 us
    all_to_all x5, blocking collectives: 74.8 us -> 72.3 us  [exchange(): return lax.all_to_all(values, axes, 0, 0, tiled=True)]
    ppermute x6 -> x7, waiting for transfers between devices: 11.9 us -> 9.57 us  [swap(): lax.ppermute(values, axis, [(n, n ^ step) for n in range(lax.axis_size(ax...]
    all_to_all x2, waiting for transfers between devices: 6.51 us -> 8.48 us  [exchange(): return lax.all_to_all(values, axes, 0, 0, tiled=True)]
    all_to_all x2, starting transfers between devices: 12.7 us -> 11.1 us  [exchange(): return lax.all_to_all(values, axes, 0, 0, tiled=True)]
    pallas_call x8 -> x10, Pallas kernels: 9.52 us -> 10.3 us  [call(): pl.pallas_call(kernel, out_shape=[jax.ShapeDtypeStruct(shape, dtype) for...]
    ppermute x6 -> x7, starting transfers between devices: 3.67 us -> 3.93 us  [swap(): lax.ppermute(values, axis, [(n, n ^ step) for n in range(lax.axis_size(ax...]
  transfers between devices with their start and end apart: 8 -> 9, of which waited for: 5 -> 4; matrix products, arithmetic and copies ran while one was open for 0% -> 0% of each run, Pallas kernels for 0% -> 4%
where the time goes in v4:
time: 117 us; the launch traced here: 116 us
  blocking collectives  72.3 us (62%)
  waiting for transfers between devices  18.1 us (15%)
  starting transfers between devices  15 us (13%)
  Pallas kernels  10.3 us (9%)
    all_to_all x5, blocking collectives, exchange(): return lax.all_to_all(values, axes, 0, 0, tiled=True)  72.3 us
    all_to_all x2, starting transfers between devices, exchange(): return lax.all_to_all(values, axes, 0, 0, tiled=True)  11.1 us
    pallas_call x10, Pallas kernels, call(): pl.pallas_call(kernel, out_shape=[jax.ShapeDtypeStruct(shape, dtype) for...  10.3 us
    ppermute x7, waiting for transfers between devices, swap(): lax.ppermute(values, axis, [(n, n ^ step) for n in range(lax.axis_size(ax...  9.57 us
    all_to_all x2, waiting for transfers between devices, exchange(): return lax.all_to_all(values, axes, 0, 0, tiled=True)  8.48 us
    ppermute x7, starting transfers between devices, swap(): lax.ppermute(values, axis, [(n, n ^ step) for n in range(lax.axis_size(ax...  3.93 us
  transfers between devices with their start and end apart: 9, of which 4 were waited for; matrix products, arithmetic and copies ran while one was open for 0% of the time, Pallas kernels for 4%

profile of v4, /device:TPU:1, one launch (start us, length us, event | category | flops | bytes accessed | tf_op | source)
XLA Modules:
  0.0 116.5 jit_solution(2504030433127616210)
XLA Ops:
  0.6 2.1 %shard_map.119 = (bf16[32,8,128]{2,1,0:T(8,128)(2,1)S(1)}, s32[8,32]{1,0:T(8,128)S(1)}, f32[1,128]{1,0:T(1,128)S(1)}, bf16[128,512]{1,0:T(8,128)(2,1)S(1)}, f32[...) custom-call(bf16[32,8,128]{2,1,0:T(8,128)(2,1)} %refs_0_.1, ...), custom_call_target="tpu_custom_call" | custom-call | tf_op jit(solution)/shard_map/pallas_call | solution.py:433
  2.8 18.9 %all_to_all.82 = bf16[16,32,128]{2,1,0:T(8,128)(2,1)S(1)} all-to-all(bf16[16,32,128]{2,1,0:T(8,128)(2,1)S(1)} %bitcast.30), channel_id=1, replica_groups=mesh['row'=8,'z'=8,'y'=2,'core'=2] {'z','core'}, dimensions={0} | all-to-all | bytes 262144 | tf_op jit(solution)/shard_map/all_to_all | solution.py:451
  21.7 0.9 shard_map.120
  22.6 6.8 %all-to-all-start.1 = ((bf16[16,128,128]{2,1,0:T(8,128)(2,1)}), bf16[16,128,128]{2,1,0:T(8,128)(2,1)S(1)}, u32[]{:S(2)}, u32[]{:S(2)}) async-start(bf16[16,128,128]{2,1,0:T(8,128)(2,1)} %bitcast.5), calls=%async_computation.1 | async-start | bytes 1048576 | tf_op jit(solution)/shard_map/all_to_all | solution.py:451
  29.4 0.7 collective-permute-start
  30.1 1.3 %collective-permute-start.1 = (bf16[128,256]{1,0:T(8,128)(2,1)S(1)}, bf16[128,256]{1,0:T(8,128)(2,1)S(1)}, u32[]{:S(2)}, u32[]{:S(2)}) collective-permute-start(bf16[128,256]{1,0:T(8,128)(2,1)S(1)} %get-tuple-element.96.own), channel_id=1, source_target_pairs={{0,2},{2,0},{1,3},{3,1},{4,6},{6,4},{5,7},{7,5},{8,10},{10,8},{9,1... | collective-permute-start | bytes 196616 | tf_op jit(solution)/shard_map/ppermute | solution.py:455
  31.4 0.4 shard_map.121
  31.7 6.5 %collective-permute-done = bf16[8,4096]{1,0:T(8,128)(2,1)S(1)} collective-permute-done((bf16[8,4096]{1,0:T(8,128)(2,1)S(1)}, bf16[8,4096]{1,0:T(8,128)(2,1)S(1)}, u32[]{:S(2)}, u32[]{:S(2)}) %collective-permute-start) | collective-permute-done | bytes 65568 | tf_op jit(solution)/shard_map/ppermute | solution.py:455
  38.2 0.0 collective-permute-done.1.near
  38.2 2.6 %all-to-all-done.1 = bf16[16,128,128]{2,1,0:T(8,128)(2,1)S(1)} async-done(((bf16[16,128,128]{2,1,0:T(8,128)(2,1)}), bf16[16,128,128]{2,1,0:T(8,128)(2,1)S(1)}, u32[]{:S(2)}, u32[]{:S(2)}) %all-to-all-start.1) | async-done | bytes 524320 | tf_op jit(solution)/shard_map/all_to_all | solution.py:451
  40.8 0.1 collective-permute-start.2
  40.9 0.5 shard_map.122
  41.4 12.8 %all_to_all.83 = bf16[16,16,128]{2,1,0:T(8,128)(2,1)S(1)} all-to-all(bf16[16,16,128]{2,1,0:T(8,128)(2,1)S(1)} %bitcast.32), channel_id=1, replica_groups=mesh['row'=8,'z'=8,'y'=2,'core'=2] {'z','core'}, dimensions={0} | all-to-all | bytes 131072 | tf_op jit(solution)/shard_map/all_to_all | solution.py:451
  54.2 0.0 collective-permute-done.2
  54.2 0.3 collective-permute-start.3
  54.5 1.1 shard_map.123
  55.6 12.5 %all_to_all.84 = bf16[16,32,128]{2,1,0:T(8,128)(2,1)S(1)} all-to-all(bf16[16,32,128]{2,1,0:T(8,128)(2,1)S(1)} %bitcast.31), channel_id=1, replica_groups=mesh['row'=8,'z'=8,'y'=2,'core'=2] {'z','core'}, dimensions={0} | all-to-all | bytes 262144 | tf_op jit(solution)/shard_map/all_to_all | solution.py:451
  68.1 0.0 collective-permute-done.3
  68.1 0.2 collective-permute-start.5
  68.3 1.5 %shard_map.124 = (f32[256,128]{1,0:T(8,128)S(1)}, bf16[256,128]{1,0:T(8,128)(2,1)S(1)}, bf16[2048,128]{1,0:T(8,128)(2,1)}) custom-call(bf16[256,256]{1,0:T(8,128)(2,1)S(1)} %get-tuple-element.108.a_all, bf16[2048,128]{1,0:T(8,128)(2,1)S(1)} %bitcast.18, bf16[512,128]{1,0:T(8,128)(2,1)S(1)} %bitcast.23), custom_call_target="tpu_custom_call" | custom-call | tf_op jit(solution)/shard_map/pallas_call | solution.py:433
  69.8 4.4 %all-to-all-start.4 = ((bf16[16,128,128]{2,1,0:T(8,128)(2,1)}), bf16[16,128,128]{2,1,0:T(8,128)(2,1)S(1)}, u32[]{:S(2)}, u32[]{:S(2)}) async-start(bf16[16,128,128]{2,1,0:T(8,128)(2,1)} %bitcast.11), calls=%async_computation.4 | async-start | bytes 1048576 | tf_op jit(solution)/shard_map/all_to_all | solution.py:451
  74.2 1.4 %collective-permute-start.4 = (bf16[256,128]{1,0:T(8,128)(2,1)S(1)}, bf16[256,128]{1,0:T(8,128)(2,1)S(1)}, u32[]{:S(2)}, u32[]{:S(2)}) collective-permute-start(bf16[256,128]{1,0:T(8,128)(2,1)S(1)} %get-tuple-element.114), channel_id=1, source_target_pairs={{0,2},{2,0},{1,3},{3,1},{4,6},{6,4},{5,7},{7,5},{8,10},{10,8},{9,1... | collective-permute-start | bytes 196616 | tf_op jit(solution)/shard_map/ppermute | solution.py:455
  75.5 3.1 %collective-permute-done.4.d_a_near = bf16[256,128]{1,0:T(8,128)(2,1)S(1)} collective-permute-done((bf16[256,128]{1,0:T(8,128)(2,1)S(1)}, bf16[256,128]{1,0:T(8,128)(2,1)S(1)}, u32[]{:S(2)}, u32[]{:S(2)}) %collective-permute-start.4) | collective-permute-done | bytes 65568 | tf_op jit(solution)/shard_map/ppermute | solution.py:455
  78.6 5.9 %all-to-all-done.4 = bf16[16,128,128]{2,1,0:T(8,128)(2,1)S(1)} async-done(((bf16[16,128,128]{2,1,0:T(8,128)(2,1)}), bf16[16,128,128]{2,1,0:T(8,128)(2,1)S(1)}, u32[]{:S(2)}, u32[]{:S(2)}) %all-to-all-start.4) | async-done | bytes 524320 | tf_op jit(solution)/shard_map/all_to_all | solution.py:451
  84.5 0.0 collective-permute-done.5.wide_1
  84.5 1.3 %shard_map.125 = (f32[256,128]{1,0:T(8,128)S(1)}, f32[256,128]{1,0:T(8,128)S(1)}, bf16[768,128]{1,0:T(8,128)(2,1)S(1)}) custom-call(bf16[64,4096]{1,0:T(8,128)(2,1)S(1)} %constant_dynamic-update-slice_fusion.4.wide_0, bf16[64,4096]{1,0:T(8,128)(2,1)S(1)} %collective-permute-done.5.wide_1, bf16[128,512]{1,0:T(8,128)(2,1)S(1)} %get-tuple-element.82.w_ab, ...), custom_call_target="tpu_custom_call" | custom-call | tf_op jit(solution)/shard_map/pallas_call | solution.py:433
  85.8 11.4 %all_to_all.85 = bf16[16,48,128]{2,1,0:T(8,128)(2,1)S(1)} all-to-all(bf16[16,48,128]{2,1,0:T(8,128)(2,1)S(1)} %bitcast.29), channel_id=1, replica_groups=mesh['row'=8,'z'=8,'y'=2,'core'=2] {'row','y'}, dimensions={0} | all-to-all | bytes 393216 | tf_op jit(solution)/shard_map/all_to_all | solution.py:451
  97.3 16.6 %all_to_all.86 = bf16[16,56,128]{2,1,0:T(8,128)(2,1)S(1)} all-to-all(bf16[16,56,128]{2,1,0:T(8,128)(2,1)S(1)} %bitcast.25), channel_id=1, replica_groups=mesh['row'=8,'z'=8,'y'=2,'core'=2] {'z','core'}, dimensions={0} | all-to-all | bytes 458752 | tf_op jit(solution)/shard_map/all_to_all | solution.py:451
  113.9 0.0 collective-permute-start.6
  114.0 1.6 %shard_map.127 = bf16[32,8,128]{2,1,0:T(8,128)(2,1)} custom-call(bf16[896,128]{1,0:T(8,128)(2,1)S(1)} %bitcast.21, s32[8,32]{1,0:T(8,128)S(1)} %get-tuple-element.125.mask, f32[1,128]{1,0:T(1,128)S(1)} %get-tuple-element.126.gain, bf16[128,128]{1,0:T(8,128)(2,1)S(1)} %get-tuple-element.85.w_gate, bf16[256,128]{1,0:T(8,128)(2,1)S(1)} %get-tuple-element.127.d_gate, ...), custom_call_target="tpu_custom_call" | custom-call | tf_op jit(solution)/shard_map/pallas_call | solution.py:433
  115.5 0.0 collective-permute-done.6.recv_near
  115.5 0.9 shard_map.128
  (7 shorter events, 0.1 us)
Async XLA Ops:
  22.6 18.2 %all-to-all-start.1 = ((bf16[16,128,128]{2,1,0:T(8,128)(2,1)}), bf16[16,128,128]{2,1,0:T(8,128)(2,1)S(1)}, u32[]{:S(2)}, u32[]{:S(2)}) async-start(bf16[16,128,128]{2,1,0:T(8,128)(2,1)} %bitcast.5), calls=%async_computation.1 | async-start | bytes 1048576 | tf_op jit(solution)/shard_map/all_to_all | solution.py:451
  29.4 8.9 %collective-permute-start = (bf16[8,4096]{1,0:T(8,128)(2,1)S(1)}, bf16[8,4096]{1,0:T(8,128)(2,1)S(1)}, u32[]{:S(2)}, u32[]{:S(2)}) collective-permute-start(bf16[8,4096]{1,0:T(8,128)(2,1)S(1)} %get-tuple-element.100), channel_id=1, source_target_pairs={{0,16},{4,20},{8,24},{12,28},{16,0},{20,4},{24,8},{28,12},{1,17},{... | collective-permute-start | bytes 196616 | tf_op jit(solution)/shard_map/ppermute | solution.py:455
  30.1 8.1 %collective-permute-start.1 = (bf16[128,256]{1,0:T(8,128)(2,1)S(1)}, bf16[128,256]{1,0:T(8,128)(2,1)S(1)}, u32[]{:S(2)}, u32[]{:S(2)}) collective-permute-start(bf16[128,256]{1,0:T(8,128)(2,1)S(1)} %get-tuple-element.96.own), channel_id=1, source_target_pairs={{0,2},{2,0},{1,3},{3,1},{4,6},{6,4},{5,7},{7,5},{8,10},{10,8},{9,1... | collective-permute-start | bytes 196616 | tf_op jit(solution)/shard_map/ppermute | solution.py:455
  40.8 13.4 %collective-permute-start.2 = (bf16[16,4096]{1,0:T(8,128)(2,1)S(1)}, bf16[16,4096]{1,0:T(8,128)(2,1)S(1)}, u32[]{:S(2)}, u32[]{:S(2)}) collective-permute-start(bf16[16,4096]{1,0:T(8,128)(2,1)S(1)} %constant_dynamic-update-slice_fusion), channel_id=1, source_target_pairs={{0,8},{4,12},{8,0},{12,4},{16,24},{20,28},{24,16},{28,20},{1,9},{5... | collective-permute-start | bytes 393224 | tf_op jit(solution)/shard_map/ppermute | solution.py:455
  54.2 13.8 %collective-permute-start.3 = (bf16[32,4096]{1,0:T(8,128)(2,1)S(1)}, bf16[32,4096]{1,0:T(8,128)(2,1)S(1)}, u32[]{:S(2)}, u32[]{:S(2)}) collective-permute-start(bf16[32,4096]{1,0:T(8,128)(2,1)S(1)} %constant_dynamic-update-slice_fusion.2), channel_id=1, source_target_pairs={{0,4},{4,0},{8,12},{12,8},{16,20},{20,16},{24,28},{28,24},{1,5},{5... | collective-permute-start | bytes 786440 | tf_op jit(solution)/shard_map/ppermute | solution.py:455
  68.1 16.4 %collective-permute-start.5 = (bf16[64,4096]{1,0:T(8,128)(2,1)S(1)}, bf16[64,4096]{1,0:T(8,128)(2,1)S(1)}, u32[]{:S(2)}, u32[]{:S(2)}) collective-permute-start(bf16[64,4096]{1,0:T(8,128)(2,1)S(1)} %constant_dynamic-update-slice_fusion.4.wide_0), channel_id=1, source_target_pairs={{0,1},{1,0},{2,3},{3,2},{4,5},{5,4},{6,7},{7,6},{8,9},{9,8},{10,11... | collective-permute-start | bytes 1572872 | tf_op jit(solution)/shard_map/ppermute | solution.py:455
  69.8 14.7 %all-to-all-start.4 = ((bf16[16,128,128]{2,1,0:T(8,128)(2,1)}), bf16[16,128,128]{2,1,0:T(8,128)(2,1)S(1)}, u32[]{:S(2)}, u32[]{:S(2)}) async-start(bf16[16,128,128]{2,1,0:T(8,128)(2,1)} %bitcast.11), calls=%async_computation.4 | async-start | bytes 1048576 | tf_op jit(solution)/shard_map/all_to_all | solution.py:451
  74.2 4.4 %collective-permute-start.4 = (bf16[256,128]{1,0:T(8,128)(2,1)S(1)}, bf16[256,128]{1,0:T(8,128)(2,1)S(1)}, u32[]{:S(2)}, u32[]{:S(2)}) collective-permute-start(bf16[256,128]{1,0:T(8,128)(2,1)S(1)} %get-tuple-element.114), channel_id=1, source_target_pairs={{0,2},{2,0},{1,3},{3,1},{4,6},{6,4},{5,7},{7,5},{8,10},{10,8},{9,1... | collective-permute-start | bytes 196616 | tf_op jit(solution)/shard_map/ppermute | solution.py:455
  113.9 1.6 %collective-permute-start.6 = (bf16[896,128]{1,0:T(8,128)(2,1)S(1)}, bf16[896,128]{1,0:T(8,128)(2,1)S(1)}, u32[]{:S(2)}, u32[]{:S(2)}) collective-permute-start(bf16[896,128]{1,0:T(8,128)(2,1)S(1)} %bitcast.20), channel_id=1, source_target_pairs={{0,1},{1,0},{2,3},{3,2},{4,5},{5,4},{6,7},{7,6},{8,9},{9,8},{10,11... | collective-permute-start | bytes 688136 | tf_op jit(solution)/shard_map/ppermute | solution.py:455

commit v5 on v4

--- a/solution.py
+++ b/solution.py
@@ -18,7 +18,7 @@
 TAPS = 4 * GROUP
 SHARE = TAPS + 2 * WIDTH // NLANE
 FINAL = 4 * COLS + SHARE // 2
-GATHER = (("z", 4), ("z", 2), ("z", 1), ("core", 1))
+GATHER = (("z", 4), ("z", 2), ("core", 1), ("z", 1))
 
 
 def dot(left, right, left_dim, right_dim):

time: 117 us -> 117 us (level)
  no operation moved by 1% of the time
where the time goes in v5:
time: 117 us; the launch traced here: 116 us
  blocking collectives  71.9 us (61%)
  waiting for transfers between devices  18.1 us (15%)
  starting transfers between devices  14.9 us (13%)
  Pallas kernels  10.3 us (9%)
    all_to_all x5, blocking collectives, exchange(): return lax.all_to_all(values, axes, 0, 0, tiled=True)  71.9 us
    all_to_all x2, starting transfers between devices, exchange(): return lax.all_to_all(values, axes, 0, 0, tiled=True)  11.1 us
    pallas_call x10, Pallas kernels, call(): pl.pallas_call(kernel, out_shape=[jax.ShapeDtypeStruct(shape, dtype) for...  10.3 us
    ppermute x7, waiting for transfers between devices, swap(): lax.ppermute(values, axis, [(n, n ^ step) for n in range(lax.axis_size(ax...  9.63 us
    all_to_all x2, waiting for transfers between devices, exchange(): return lax.all_to_all(values, axes, 0, 0, tiled=True)  8.44 us
    ppermute x7, starting transfers between devices, swap(): lax.ppermute(values, axis, [(n, n ^ step) for n in range(lax.axis_size(ax...  3.81 us
  transfers between devices with their start and end apart: 9, of which 4 were waited for; matrix products, arithmetic and copies ran while one was open for 0% of the time, Pallas kernels for 4%

profile of v5, /device:TPU:1, one launch (start us, length us, event | category | flops | bytes accessed | tf_op | source)
XLA Modules:
  0.0 116.0 jit_solution(2927929841312261074)
XLA Ops:
  0.6 2.1 %shard_map.119 = (bf16[32,8,128]{2,1,0:T(8,128)(2,1)S(1)}, s32[8,32]{1,0:T(8,128)S(1)}, f32[1,128]{1,0:T(1,128)S(1)}, bf16[128,512]{1,0:T(8,128)(2,1)S(1)}, f32[...) custom-call(bf16[32,8,128]{2,1,0:T(8,128)(2,1)} %refs_0_.1, ...), custom_call_target="tpu_custom_call" | custom-call | tf_op jit(solution)/shard_map/pallas_call | solution.py:433
  2.8 18.9 %all_to_all.82 = bf16[16,32,128]{2,1,0:T(8,128)(2,1)S(1)} all-to-all(bf16[16,32,128]{2,1,0:T(8,128)(2,1)S(1)} %bitcast.30), channel_id=1, replica_groups=mesh['row'=8,'z'=8,'y'=2,'core'=2] {'z','core'}, dimensions={0} | all-to-all | bytes 262144 | tf_op jit(solution)/shard_map/all_to_all | solution.py:451
  21.7 0.9 shard_map.120
  22.6 6.8 %all-to-all-start.1 = ((bf16[16,128,128]{2,1,0:T(8,128)(2,1)}), bf16[16,128,128]{2,1,0:T(8,128)(2,1)S(1)}, u32[]{:S(2)}, u32[]{:S(2)}) async-start(bf16[16,128,128]{2,1,0:T(8,128)(2,1)} %bitcast.5), calls=%async_computation.1 | async-start | bytes 1048576 | tf_op jit(solution)/shard_map/all_to_all | solution.py:451
  29.4 0.7 collective-permute-start
  30.1 1.3 %collective-permute-start.1 = (bf16[128,256]{1,0:T(8,128)(2,1)S(1)}, bf16[128,256]{1,0:T(8,128)(2,1)S(1)}, u32[]{:S(2)}, u32[]{:S(2)}) collective-permute-start(bf16[128,256]{1,0:T(8,128)(2,1)S(1)} %get-tuple-element.96.own), channel_id=1, source_target_pairs={{0,2},{2,0},{1,3},{3,1},{4,6},{6,4},{5,7},{7,5},{8,10},{10,8},{9,1... | collective-permute-start | bytes 196616 | tf_op jit(solution)/shard_map/ppermute | solution.py:455
  31.4 0.4 shard_map.121
  31.7 6.5 %collective-permute-done = bf16[8,4096]{1,0:T(8,128)(2,1)S(1)} collective-permute-done((bf16[8,4096]{1,0:T(8,128)(2,1)S(1)}, bf16[8,4096]{1,0:T(8,128)(2,1)S(1)}, u32[]{:S(2)}, u32[]{:S(2)}) %collective-permute-start) | collective-permute-done | bytes 65568 | tf_op jit(solution)/shard_map/ppermute | solution.py:455
  38.2 0.0 collective-permute-done.1.near
  38.2 2.6 %all-to-all-done.1 = bf16[16,128,128]{2,1,0:T(8,128)(2,1)S(1)} async-done(((bf16[16,128,128]{2,1,0:T(8,128)(2,1)}), bf16[16,128,128]{2,1,0:T(8,128)(2,1)S(1)}, u32[]{:S(2)}, u32[]{:S(2)}) %all-to-all-start.1) | async-done | bytes 524320 | tf_op jit(solution)/shard_map/all_to_all | solution.py:451
  40.8 0.1 collective-permute-start.2
  40.9 0.5 shard_map.122
  41.4 12.8 %all_to_all.83 = bf16[16,16,128]{2,1,0:T(8,128)(2,1)S(1)} all-to-all(bf16[16,16,128]{2,1,0:T(8,128)(2,1)S(1)} %bitcast.32), channel_id=1, replica_groups=mesh['row'=8,'z'=8,'y'=2,'core'=2] {'z','core'}, dimensions={0} | all-to-all | bytes 131072 | tf_op jit(solution)/shard_map/all_to_all | solution.py:451
  54.2 0.0 collective-permute-done.2
  54.2 0.2 collective-permute-start.3
  54.5 1.1 shard_map.123
  55.6 12.0 %all_to_all.84 = bf16[16,32,128]{2,1,0:T(8,128)(2,1)S(1)} all-to-all(bf16[16,32,128]{2,1,0:T(8,128)(2,1)S(1)} %bitcast.31), channel_id=1, replica_groups=mesh['row'=8,'z'=8,'y'=2,'core'=2] {'z','core'}, dimensions={0} | all-to-all | bytes 262144 | tf_op jit(solution)/shard_map/all_to_all | solution.py:451
  67.5 0.0 collective-permute-done.3
  67.6 0.1 collective-permute-start.5
  67.7 1.5 %shard_map.124 = (f32[256,128]{1,0:T(8,128)S(1)}, bf16[256,128]{1,0:T(8,128)(2,1)S(1)}, bf16[2048,128]{1,0:T(8,128)(2,1)}) custom-call(bf16[256,256]{1,0:T(8,128)(2,1)S(1)} %get-tuple-element.108.a_all, bf16[2048,128]{1,0:T(8,128)(2,1)S(1)} %bitcast.18, bf16[512,128]{1,0:T(8,128)(2,1)S(1)} %bitcast.23), custom_call_target="tpu_custom_call" | custom-call | tf_op jit(solution)/shard_map/pallas_call | solution.py:433
  69.2 4.4 %all-to-all-start.4 = ((bf16[16,128,128]{2,1,0:T(8,128)(2,1)}), bf16[16,128,128]{2,1,0:T(8,128)(2,1)S(1)}, u32[]{:S(2)}, u32[]{:S(2)}) async-start(bf16[16,128,128]{2,1,0:T(8,128)(2,1)} %bitcast.11), calls=%async_computation.4 | async-start | bytes 1048576 | tf_op jit(solution)/shard_map/all_to_all | solution.py:451
  73.6 1.4 %collective-permute-start.4 = (bf16[256,128]{1,0:T(8,128)(2,1)S(1)}, bf16[256,128]{1,0:T(8,128)(2,1)S(1)}, u32[]{:S(2)}, u32[]{:S(2)}) collective-permute-start(bf16[256,128]{1,0:T(8,128)(2,1)S(1)} %get-tuple-element.114), channel_id=1, source_target_pairs={{0,2},{2,0},{1,3},{3,1},{4,6},{6,4},{5,7},{7,5},{8,10},{10,8},{9,1... | collective-permute-start | bytes 196616 | tf_op jit(solution)/shard_map/ppermute | solution.py:455
  74.9 3.1 %collective-permute-done.4.d_a_near = bf16[256,128]{1,0:T(8,128)(2,1)S(1)} collective-permute-done((bf16[256,128]{1,0:T(8,128)(2,1)S(1)}, bf16[256,128]{1,0:T(8,128)(2,1)S(1)}, u32[]{:S(2)}, u32[]{:S(2)}) %collective-permute-start.4) | collective-permute-done | bytes 65568 | tf_op jit(solution)/shard_map/ppermute | solution.py:455
  78.0 5.9 %all-to-all-done.4 = bf16[16,128,128]{2,1,0:T(8,128)(2,1)S(1)} async-done(((bf16[16,128,128]{2,1,0:T(8,128)(2,1)}), bf16[16,128,128]{2,1,0:T(8,128)(2,1)S(1)}, u32[]{:S(2)}, u32[]{:S(2)}) %all-to-all-start.4) | async-done | bytes 524320 | tf_op jit(solution)/shard_map/all_to_all | solution.py:451
  83.9 0.0 collective-permute-done.5.wide_1
  83.9 1.3 %shard_map.125 = (f32[256,128]{1,0:T(8,128)S(1)}, f32[256,128]{1,0:T(8,128)S(1)}, bf16[768,128]{1,0:T(8,128)(2,1)S(1)}) custom-call(bf16[64,4096]{1,0:T(8,128)(2,1)S(1)} %constant_dynamic-update-slice_fusion.4.wide_0, bf16[64,4096]{1,0:T(8,128)(2,1)S(1)} %collective-permute-done.5.wide_1, bf16[128,512]{1,0:T(8,128)(2,1)S(1)} %get-tuple-element.82.w_ab, ...), custom_call_target="tpu_custom_call" | custom-call | tf_op jit(solution)/shard_map/pallas_call | solution.py:433
  85.3 11.4 %all_to_all.85 = bf16[16,48,128]{2,1,0:T(8,128)(2,1)S(1)} all-to-all(bf16[16,48,128]{2,1,0:T(8,128)(2,1)S(1)} %bitcast.29), channel_id=1, replica_groups=mesh['row'=8,'z'=8,'y'=2,'core'=2] {'row','y'}, dimensions={0} | all-to-all | bytes 393216 | tf_op jit(solution)/shard_map/all_to_all | solution.py:451
  96.7 16.8 %all_to_all.86 = bf16[16,56,128]{2,1,0:T(8,128)(2,1)S(1)} all-to-all(bf16[16,56,128]{2,1,0:T(8,128)(2,1)S(1)} %bitcast.25), channel_id=1, replica_groups=mesh['row'=8,'z'=8,'y'=2,'core'=2] {'z','core'}, dimensions={0} | all-to-all | bytes 458752 | tf_op jit(solution)/shard_map/all_to_all | solution.py:451
  113.5 0.0 collective-permute-start.6
  113.5 1.6 %shard_map.127 = bf16[32,8,128]{2,1,0:T(8,128)(2,1)} custom-call(bf16[896,128]{1,0:T(8,128)(2,1)S(1)} %bitcast.21, s32[8,32]{1,0:T(8,128)S(1)} %get-tuple-element.125.mask, f32[1,128]{1,0:T(1,128)S(1)} %get-tuple-element.126.gain, bf16[128,128]{1,0:T(8,128)(2,1)S(1)} %get-tuple-element.85.w_gate, bf16[256,128]{1,0:T(8,128)(2,1)S(1)} %get-tuple-element.127.d_gate, ...), custom_call_target="tpu_custom_call" | custom-call | tf_op jit(solution)/shard_map/pallas_call | solution.py:433
  115.1 0.0 collective-permute-done.6.recv_near
  115.1 0.9 shard_map.128
  (7 shorter events, 0.1 us)
Async XLA Ops:
  22.6 18.2 %all-to-all-start.1 = ((bf16[16,128,128]{2,1,0:T(8,128)(2,1)}), bf16[16,128,128]{2,1,0:T(8,128)(2,1)S(1)}, u32[]{:S(2)}, u32[]{:S(2)}) async-start(bf16[16,128,128]{2,1,0:T(8,128)(2,1)} %bitcast.5), calls=%async_computation.1 | async-start | bytes 1048576 | tf_op jit(solution)/shard_map/all_to_all | solution.py:451
  29.4 8.9 %collective-permute-start = (bf16[8,4096]{1,0:T(8,128)(2,1)S(1)}, bf16[8,4096]{1,0:T(8,128)(2,1)S(1)}, u32[]{:S(2)}, u32[]{:S(2)}) collective-permute-start(bf16[8,4096]{1,0:T(8,128)(2,1)S(1)} %get-tuple-element.100), channel_id=1, source_target_pairs={{0,16},{4,20},{8,24},{12,28},{16,0},{20,4},{24,8},{28,12},{1,17},{... | collective-permute-start | bytes 196616 | tf_op jit(solution)/shard_map/ppermute | solution.py:455
  30.1 8.1 %collective-permute-start.1 = (bf16[128,256]{1,0:T(8,128)(2,1)S(1)}, bf16[128,256]{1,0:T(8,128)(2,1)S(1)}, u32[]{:S(2)}, u32[]{:S(2)}) collective-permute-start(bf16[128,256]{1,0:T(8,128)(2,1)S(1)} %get-tuple-element.96.own), channel_id=1, source_target_pairs={{0,2},{2,0},{1,3},{3,1},{4,6},{6,4},{5,7},{7,5},{8,10},{10,8},{9,1... | collective-permute-start | bytes 196616 | tf_op jit(solution)/shard_map/ppermute | solution.py:455
  40.8 13.4 %collective-permute-start.2 = (bf16[16,4096]{1,0:T(8,128)(2,1)S(1)}, bf16[16,4096]{1,0:T(8,128)(2,1)S(1)}, u32[]{:S(2)}, u32[]{:S(2)}) collective-permute-start(bf16[16,4096]{1,0:T(8,128)(2,1)S(1)} %constant_dynamic-update-slice_fusion), channel_id=1, source_target_pairs={{0,8},{4,12},{8,0},{12,4},{16,24},{20,28},{24,16},{28,20},{1,9},{5... | collective-permute-start | bytes 393224 | tf_op jit(solution)/shard_map/ppermute | solution.py:455
  54.2 13.3 %collective-permute-start.3 = (bf16[32,4096]{1,0:T(8,128)(2,1)S(1)}, bf16[32,4096]{1,0:T(8,128)(2,1)S(1)}, u32[]{:S(2)}, u32[]{:S(2)}) collective-permute-start(bf16[32,4096]{1,0:T(8,128)(2,1)S(1)} %constant_dynamic-update-slice_fusion.2), channel_id=1, source_target_pairs={{0,1},{1,0},{2,3},{3,2},{4,5},{5,4},{6,7},{7,6},{8,9},{9,8},{10,11... | collective-permute-start | bytes 786440 | tf_op jit(solution)/shard_map/ppermute | solution.py:455
  67.6 16.3 %collective-permute-start.5 = (bf16[64,4096]{1,0:T(8,128)(2,1)S(1)}, bf16[64,4096]{1,0:T(8,128)(2,1)S(1)}, u32[]{:S(2)}, u32[]{:S(2)}) collective-permute-start(bf16[64,4096]{1,0:T(8,128)(2,1)S(1)} %constant_dynamic-update-slice_fusion.4.wide_0), channel_id=1, source_target_pairs={{0,4},{4,0},{8,12},{12,8},{16,20},{20,16},{24,28},{28,24},{1,5},{5... | collective-permute-start | bytes 1572872 | tf_op jit(solution)/shard_map/ppermute | solution.py:455
  69.2 14.7 %all-to-all-start.4 = ((bf16[16,128,128]{2,1,0:T(8,128)(2,1)}), bf16[16,128,128]{2,1,0:T(8,128)(2,1)S(1)}, u32[]{:S(2)}, u32[]{:S(2)}) async-start(bf16[16,128,128]{2,1,0:T(8,128)(2,1)} %bitcast.11), calls=%async_computation.4 | async-start | bytes 1048576 | tf_op jit(solution)/shard_map/all_to_all | solution.py:451
  73.6 4.5 %collective-permute-start.4 = (bf16[256,128]{1,0:T(8,128)(2,1)S(1)}, bf16[256,128]{1,0:T(8,128)(2,1)S(1)}, u32[]{:S(2)}, u32[]{:S(2)}) collective-permute-start(bf16[256,128]{1,0:T(8,128)(2,1)S(1)} %get-tuple-element.114), channel_id=1, source_target_pairs={{0,2},{2,0},{1,3},{3,1},{4,6},{6,4},{5,7},{7,5},{8,10},{10,8},{9,1... | collective-permute-start | bytes 196616 | tf_op jit(solution)/shard_map/ppermute | solution.py:455
  113.5 1.6 %collective-permute-start.6 = (bf16[896,128]{1,0:T(8,128)(2,1)S(1)}, bf16[896,128]{1,0:T(8,128)(2,1)S(1)}, u32[]{:S(2)}, u32[]{:S(2)}) collective-permute-start(bf16[896,128]{1,0:T(8,128)(2,1)S(1)} %bitcast.20), channel_id=1, source_target_pairs={{0,1},{1,0},{2,3},{3,2},{4,5},{5,4},{6,7},{7,6},{8,9},{9,8},{10,11... | collective-permute-start | bytes 688136 | tf_op jit(solution)/shard_map/ppermute | solution.py:455

commit v6 on v5

--- a/solution.py
+++ b/solution.py
@@ -144,9 +144,9 @@
     ]
     for copy in copies:
         copy.start()
-    for copy in copies:
+    pair_here, mask_here, gain_here, w_here = kept[:4]
+    for copy in copies[:3]:
         copy.wait()
-    pair_here, mask_here, gain_here, w_here = kept[:4]
     h_in, _ = layer_norm(pair_here[...].astype(F32).reshape(PAIRS, WIDTH), 1)
     rows[...] = (h_in * gain_here[...]).astype(BF16).astype(F32)
     normed = jnp.concatenate(
@@ -157,6 +157,7 @@
     wide_out[...] = jnp.concatenate(
         [rows[i * COLS : (i + 1) * COLS] * flags[:, i : i + 1] for i in range(ROWS)], axis=1
     ).astype(BF16)
+    copies[3].wait()
     weights[...] = w_here[...].astype(F32).T
     proj = dot(regroup(weights, 4).astype(BF16), normed, 1, 1)
     a_val = jax.nn.sigmoid(proj[0:128]) * proj[128:256]
@@ -170,6 +171,8 @@
                 to_message(b_val, k, part, HALF) * half_flags[part][k : k + 1]
             )
     send[...] = message[...].astype(BF16)
+    for copy in copies[4:]:
+        copy.wait()
 
 
 def spread_kernel(recv, send, a_own):
@@ -185,7 +188,7 @@
     a_val = [jnp.where(is_first, own, near), jnp.where(is_first, near, own)]
     a_all[...] = jnp.concatenate(a_val, axis=0)
     block = lane_block((HALF, WIDTH))
-    pieces = []
+    pieces = [[], []]
     for r in range(NROW):
         full = None
         for y in range(2):
@@ -200,8 +203,9 @@
                 part = full[row : row + HALF, h * WIDTH : (h + 1) * WIDTH]
                 mixed = part if mixed is None else jnp.where(block == c4, part, mixed)
             found.append(mixed)
-        pieces += [found[h][core * COLS : (core + 1) * COLS] for core in range(2) for h in range(2)]
-    send[...] = jnp.concatenate(pieces, axis=0).astype(BF16)
+        for core in range(2):
+            pieces[core] += [found[h][core * COLS : (core + 1) * COLS] for h in range(2)]
+    send[...] = jnp.concatenate(pieces[0] + pieces[1], axis=0).astype(BF16)
 
 
 def prepare_kernel(
@@ -271,7 +275,9 @@
     for r in range(NROW):
         tiles = []
         for h in range(2):
-            part = d_mixed[h][r * HALF : (r + 1) * HALF]
+            part = jnp.concatenate(
+                [d_mixed[h][at : at + COLS] for at in (r * COLS, (NROW + r) * COLS)], axis=0
+            )
             nothing = jnp.zeros_like(part)
             tiles.append(
                 jnp.concatenate(
@@ -303,14 +309,14 @@
         values = jnp.where((lane >> bit) & 1 == 1, swapped, pairs).reshape(WIDTH, WIDTH)
     places = [0]
     for axis, step in GATHER:
-        places += [place ^ (2 * step if axis == "z" else step) for place in places]
+        places += [place ^ (step if axis == "z" else 8 * step) for place in places]
     return jnp.concatenate([values[p * COLS : (p + 1) * COLS] for p in places], axis=0)
 
 
 def weight_kernel(
     wide_0, wide_1, w_ab, d_a_own, d_a_near, d_b, recv_d, d_a_sum, d_b_sum, send, proj, d_proj
 ):
-    lane = lax.axis_index("z") * 2 + lax.axis_index("core")
+    lane = lax.axis_index("core") * 8 + lax.axis_index("z")
     d_a = d_a_own[...] + d_a_near[...].astype(F32)
     d_a_sum[...] = d_a
     totals = []
@@ -375,7 +381,7 @@
         for part in range(2)
     ]
     shares = jnp.broadcast_to(
-        total.reshape(1, 2, SHARE // 2, WIDTH), (NLANE // 2, 2, SHARE // 2, WIDTH)
+        total.reshape(2, 1, SHARE // 2, WIDTH), (2, NLANE // 2, SHARE // 2, WIDTH)
     )
     pieces.append(shares.reshape(NLANE, SHARE // 2, WIDTH))
     send[...] = jnp.concatenate(pieces, axis=1).reshape(NLANE * FINAL, WIDTH).astype(BF16)
@@ -409,7 +415,9 @@
     store_pairs(norm_back(d_in * gain[...], h_in[...], inv_in[...], 1), rows, grad_pair)
 
 
-def sums_kernel(recv, recv_near, grad_ab, grad_gate, grad_out, weights, message):
+def sums_kernel(
+    recv, recv_near, grad_ab, grad_gate, grad_out, weights, message, turned, others, sems
+):
     own, near = (
         part[...].astype(F32).reshape(NLANE, FINAL, WIDTH)[:, 4 * COLS :]
         for part in (recv, recv_near)
@@ -417,19 +425,27 @@
     is_first = lax.axis_index("core") == 0
     both = [jnp.where(is_first, own, near), jnp.where(is_first, near, own)]
     both = jnp.concatenate(both, axis=1)
+    others[...] = both[:, TAPS:].reshape(PAIRS, WIDTH)
+    copies = [
+        pltpu.make_async_copy(others.at[pl.ds(0, WIDTH)], grad_gate, sems.at[0]),
+        pltpu.make_async_copy(others.at[pl.ds(WIDTH, WIDTH)], grad_out, sems.at[1]),
+        pltpu.make_async_copy(turned, grad_ab, sems.at[2]),
+    ]
+    copies[0].start()
+    copies[1].start()
     message[...] = both.reshape(NLANE * SHARE, WIDTH)
     for blk in range(4):
         for cc in range(GROUP):
             weights[pl.ds(blk * WIDTH + cc, NLANE, stride=GROUP), :] = message[
                 pl.ds(blk * GROUP + cc, NLANE, stride=SHARE), :
             ]
-    grad_ab[...] = weights[...].T
-    others = both[:, TAPS:].reshape(PAIRS, WIDTH)
-    grad_gate[...] = others[:WIDTH]
-    grad_out[...] = others[WIDTH:]
-
-
-def call(kernel, outs, scratch, *args, places=None, cost=None):
+    turned[...] = weights[...].T
+    copies[2].start()
+    for copy in copies:
+        copy.wait()
+
+
+def call(kernel, outs, scratch, *args, places=None, cost=None, apart=False):
     return pl.pallas_call(
         kernel,
         out_shape=[jax.ShapeDtypeStruct(shape, dtype) for shape, dtype in outs],
@@ -437,13 +453,14 @@
             pl.BlockSpec(memory_space=pltpu.VMEM if places is None else places[n])
             for n in range(len(args))
         ],
+        out_specs=[pl.BlockSpec(memory_space=pl.ANY if apart else pltpu.VMEM) for _ in outs],
         scratch_shapes=scratch,
         compiler_params=pltpu.CompilerParams(vmem_limit_bytes=32 * 1024 * 1024),
         cost_estimate=cost,
     )(*args)
 
 
-LANES = ("z", "core")
+LANES = ("core", "z")
 SIDES = ("row", "y")
 
 
@@ -546,8 +563,15 @@
     grad_ab, grad_gate, grad_out = call(
         sums_kernel,
         [(wide, F32), (square, F32), (square, F32)],
-        [pltpu.VMEM(tall, F32), pltpu.VMEM((NLANE * SHARE, WIDTH), F32)],
+        [
+            pltpu.VMEM(tall, F32),
+            pltpu.VMEM((NLANE * SHARE, WIDTH), F32),
+            pltpu.VMEM(wide, F32),
+            pltpu.VMEM(flat, F32),
+            pltpu.SemaphoreType.DMA((3,)),
+        ],
         recv_last, recv_near,
+        apart=True,
     )
     return update, grad_pair, grad_ab, grad_gate, grad_out
 

time: 117 us -> 115 us (0.983)
  starting transfers between devices: 14.9 us -> 21.3 us
  waiting for transfers between devices: 18.1 us -> 13.8 us
  blocking collectives: 71.9 us -> 68.4 us
    ppermute x7, starting transfers between devices: 3.81 us -> 10.2 us  [swap(): lax.ppermute(values, axis, [(n, n ^ step) for n in range(lax.axis_size(ax...]
    all_to_all x2, waiting for transfers between devices: 8.44 us -> 4.9 us  [exchange(): return lax.all_to_all(values, axes, 0, 0, tiled=True)]
    all_to_all x5, blocking collectives: 71.9 us -> 68.4 us  [exchange(): return lax.all_to_all(values, axes, 0, 0, tiled=True)]
where the time goes in v6:
time: 115 us
  blocking collectives  68.4 us (59%)
  starting transfers between devices  21.3 us (19%)
  waiting for transfers between devices  13.8 us (12%)
  Pallas kernels  10.2 us (9%)
    all_to_all x5, blocking collectives, exchange(): return lax.all_to_all(values, axes, 0, 0, tiled=True)  68.4 us
    all_to_all x2, starting transfers between devices, exchange(): return lax.all_to_all(values, axes, 0, 0, tiled=True)  11.1 us
    pallas_call x10, Pallas kernels, call(): pl.pallas_call(kernel, out_shape=[jax.ShapeDtypeStruct(shape, dtype) for...  10.2 us
    ppermute x7, starting transfers between devices, swap(): lax.ppermute(values, axis, [(n, n ^ step) for n in range(lax.axis_size(ax...  10.2 us
    ppermute x7, waiting for transfers between devices, swap(): lax.ppermute(values, axis, [(n, n ^ step) for n in range(lax.axis_size(ax...  8.91 us
    all_to_all x2, waiting for transfers between devices, exchange(): return lax.all_to_all(values, axes, 0, 0, tiled=True)  4.9 us
  transfers between devices with their start and end apart: 9, of which 4 were waited for; matrix products, arithmetic and copies ran while one was open for 0% of the time, Pallas kernels for 4%

profile of v6, /device:TPU:1, one launch (start us, length us, event | category | flops | bytes accessed | tf_op | source)
XLA Modules:
  0.0 114.5 jit_solution(6968425870916961610)
XLA Ops:
  0.6 2.0 %shard_map.119 = (bf16[32,8,128]{2,1,0:T(8,128)(2,1)S(1)}, s32[8,32]{1,0:T(8,128)S(1)}, f32[1,128]{1,0:T(1,128)S(1)}, bf16[128,512]{1,0:T(8,128)(2,1)S(1)}, f32[...) custom-call(bf16[32,8,128]{2,1,0:T(8,128)(2,1)} %refs_0_.1, ...), custom_call_target="tpu_custom_call" | custom-call | tf_op jit(solution)/shard_map/pallas_call | solution.py:449
  2.6 17.1 %all_to_all.82 = bf16[16,32,128]{2,1,0:T(8,128)(2,1)S(1)} all-to-all(bf16[16,32,128]{2,1,0:T(8,128)(2,1)S(1)} %bitcast.30), channel_id=1, replica_groups=mesh['row'=8,'z'=8,'y'=2,'core'=2] {'core','z'}, dimensions={0} | all-to-all | bytes 262144 | tf_op jit(solution)/shard_map/all_to_all | solution.py:468
  19.7 0.9 shard_map.120
  20.6 6.8 %all-to-all-start.1 = ((bf16[16,128,128]{2,1,0:T(8,128)(2,1)}), bf16[16,128,128]{2,1,0:T(8,128)(2,1)S(1)}, u32[]{:S(2)}, u32[]{:S(2)}) async-start(bf16[16,128,128]{2,1,0:T(8,128)(2,1)} %bitcast.5), calls=%async_computation.1 | async-start | bytes 1048576 | tf_op jit(solution)/shard_map/all_to_all | solution.py:468
  27.4 2.4 %collective-permute-start = (bf16[8,4096]{1,0:T(8,128)(2,1)S(1)}, bf16[8,4096]{1,0:T(8,128)(2,1)S(1)}, u32[]{:S(2)}, u32[]{:S(2)}) collective-permute-start(bf16[8,4096]{1,0:T(8,128)(2,1)S(1)} %get-tuple-element.100), channel_id=1, source_target_pairs={{0,16},{4,20},{8,24},{12,28},{16,0},{20,4},{24,8},{28,12},{1,17},{... | collective-permute-start | bytes 196616 | tf_op jit(solution)/shard_map/ppermute | solution.py:472
  29.7 1.3 %collective-permute-start.1 = (bf16[128,256]{1,0:T(8,128)(2,1)S(1)}, bf16[128,256]{1,0:T(8,128)(2,1)S(1)}, u32[]{:S(2)}, u32[]{:S(2)}) collective-permute-start(bf16[128,256]{1,0:T(8,128)(2,1)S(1)} %get-tuple-element.96.own), channel_id=1, source_target_pairs={{0,2},{2,0},{1,3},{3,1},{4,6},{6,4},{5,7},{7,5},{8,10},{10,8},{9,1... | collective-permute-start | bytes 196616 | tf_op jit(solution)/shard_map/ppermute | solution.py:472
  31.0 0.4 shard_map.121
  31.4 3.2 %collective-permute-done = bf16[8,4096]{1,0:T(8,128)(2,1)S(1)} collective-permute-done((bf16[8,4096]{1,0:T(8,128)(2,1)S(1)}, bf16[8,4096]{1,0:T(8,128)(2,1)S(1)}, u32[]{:S(2)}, u32[]{:S(2)}) %collective-permute-start) | collective-permute-done | bytes 65568 | tf_op jit(solution)/shard_map/ppermute | solution.py:472
  34.6 2.8 %collective-permute-done.1.near = bf16[128,256]{1,0:T(8,128)(2,1)S(1)} collective-permute-done((bf16[128,256]{1,0:T(8,128)(2,1)S(1)}, bf16[128,256]{1,0:T(8,128)(2,1)S(1)}, u32[]{:S(2)}, u32[]{:S(2)}) %collective-permute-start.1) | collective-permute-done | bytes 65568 | tf_op jit(solution)/shard_map/ppermute | solution.py:472
  37.4 0.0 all-to-all-done.1
  37.4 1.8 %collective-permute-start.2 = (bf16[16,4096]{1,0:T(8,128)(2,1)S(1)}, bf16[16,4096]{1,0:T(8,128)(2,1)S(1)}, u32[]{:S(2)}, u32[]{:S(2)}) collective-permute-start(bf16[16,4096]{1,0:T(8,128)(2,1)S(1)} %constant_dynamic-update-slice_fusion), channel_id=1, source_target_pairs={{0,8},{4,12},{8,0},{12,4},{16,24},{20,28},{24,16},{28,20},{1,9},{5... | collective-permute-start | bytes 393224 | tf_op jit(solution)/shard_map/ppermute | solution.py:472
  39.3 0.5 shard_map.122
  39.7 13.7 %all_to_all.83 = bf16[16,16,128]{2,1,0:T(8,128)(2,1)S(1)} all-to-all(bf16[16,16,128]{2,1,0:T(8,128)(2,1)S(1)} %bitcast.32), channel_id=1, replica_groups=mesh['row'=8,'z'=8,'y'=2,'core'=2] {'core','z'}, dimensions={0} | all-to-all | bytes 131072 | tf_op jit(solution)/shard_map/all_to_all | solution.py:468
  53.5 0.0 collective-permute-done.2
  53.5 1.0 collective-permute-start.3
  54.5 1.1 shard_map.123
  55.6 9.8 %all_to_all.84 = bf16[16,32,128]{2,1,0:T(8,128)(2,1)S(1)} all-to-all(bf16[16,32,128]{2,1,0:T(8,128)(2,1)S(1)} %bitcast.31), channel_id=1, replica_groups=mesh['row'=8,'z'=8,'y'=2,'core'=2] {'core','z'}, dimensions={0} | all-to-all | bytes 262144 | tf_op jit(solution)/shard_map/all_to_all | solution.py:468
  65.4 0.0 collective-permute-done.3
  65.4 1.5 %collective-permute-start.5 = (bf16[64,4096]{1,0:T(8,128)(2,1)S(1)}, bf16[64,4096]{1,0:T(8,128)(2,1)S(1)}, u32[]{:S(2)}, u32[]{:S(2)}) collective-permute-start(bf16[64,4096]{1,0:T(8,128)(2,1)S(1)} %constant_dynamic-update-slice_fusion.4.wide_0), channel_id=1, source_target_pairs={{0,4},{4,0},{8,12},{12,8},{16,20},{20,16},{24,28},{28,24},{1,5},{5... | collective-permute-start | bytes 1572872 | tf_op jit(solution)/shard_map/ppermute | solution.py:472
  67.0 1.5 %shard_map.124 = (f32[256,128]{1,0:T(8,128)S(1)}, bf16[256,128]{1,0:T(8,128)(2,1)S(1)}, bf16[2048,128]{1,0:T(8,128)(2,1)}) custom-call(bf16[256,256]{1,0:T(8,128)(2,1)S(1)} %get-tuple-element.108.a_all, bf16[2048,128]{1,0:T(8,128)(2,1)S(1)} %bitcast.18, bf16[512,128]{1,0:T(8,128)(2,1)S(1)} %bitcast.23), custom_call_target="tpu_custom_call" | custom-call | tf_op jit(solution)/shard_map/pallas_call | solution.py:449
  68.5 4.4 %all-to-all-start.4 = ((bf16[16,128,128]{2,1,0:T(8,128)(2,1)}), bf16[16,128,128]{2,1,0:T(8,128)(2,1)S(1)}, u32[]{:S(2)}, u32[]{:S(2)}) async-start(bf16[16,128,128]{2,1,0:T(8,128)(2,1)} %bitcast.11), calls=%async_computation.4 | async-start | bytes 1048576 | tf_op jit(solution)/shard_map/all_to_all | solution.py:468
  72.9 1.4 %collective-permute-start.4 = (bf16[256,128]{1,0:T(8,128)(2,1)S(1)}, bf16[256,128]{1,0:T(8,128)(2,1)S(1)}, u32[]{:S(2)}, u32[]{:S(2)}) collective-permute-start(bf16[256,128]{1,0:T(8,128)(2,1)S(1)} %get-tuple-element.114), channel_id=1, source_target_pairs={{0,2},{2,0},{1,3},{3,1},{4,6},{6,4},{5,7},{7,5},{8,10},{10,8},{9,1... | collective-permute-start | bytes 196616 | tf_op jit(solution)/shard_map/ppermute | solution.py:472
  74.2 2.9 %collective-permute-done.4.d_a_near = bf16[256,128]{1,0:T(8,128)(2,1)S(1)} collective-permute-done((bf16[256,128]{1,0:T(8,128)(2,1)S(1)}, bf16[256,128]{1,0:T(8,128)(2,1)S(1)}, u32[]{:S(2)}, u32[]{:S(2)}) %collective-permute-start.4) | collective-permute-done | bytes 65568 | tf_op jit(solution)/shard_map/ppermute | solution.py:472
  77.1 4.9 %all-to-all-done.4 = bf16[16,128,128]{2,1,0:T(8,128)(2,1)S(1)} async-done(((bf16[16,128,128]{2,1,0:T(8,128)(2,1)}), bf16[16,128,128]{2,1,0:T(8,128)(2,1)S(1)}, u32[]{:S(2)}, u32[]{:S(2)}) %all-to-all-start.4) | async-done | bytes 524320 | tf_op jit(solution)/shard_map/all_to_all | solution.py:468
  82.0 0.0 collective-permute-done.5.wide_1
  82.0 1.3 %shard_map.125 = (f32[256,128]{1,0:T(8,128)S(1)}, f32[256,128]{1,0:T(8,128)S(1)}, bf16[768,128]{1,0:T(8,128)(2,1)S(1)}) custom-call(bf16[64,4096]{1,0:T(8,128)(2,1)S(1)} %constant_dynamic-update-slice_fusion.4.wide_0, bf16[64,4096]{1,0:T(8,128)(2,1)S(1)} %collective-permute-done.5.wide_1, bf16[128,512]{1,0:T(8,128)(2,1)S(1)} %get-tuple-element.82.w_ab, ...), custom_call_target="tpu_custom_call" | custom-call | tf_op jit(solution)/shard_map/pallas_call | solution.py:449
  83.3 11.5 %all_to_all.85 = bf16[16,48,128]{2,1,0:T(8,128)(2,1)S(1)} all-to-all(bf16[16,48,128]{2,1,0:T(8,128)(2,1)S(1)} %bitcast.29), channel_id=1, replica_groups=mesh['row'=8,'z'=8,'y'=2,'core'=2] {'row','y'}, dimensions={0} | all-to-all | bytes 393216 | tf_op jit(solution)/shard_map/all_to_all | solution.py:468
  94.9 16.2 %all_to_all.86 = bf16[16,56,128]{2,1,0:T(8,128)(2,1)S(1)} all-to-all(bf16[16,56,128]{2,1,0:T(8,128)(2,1)S(1)} %bitcast.25), channel_id=1, replica_groups=mesh['row'=8,'z'=8,'y'=2,'core'=2] {'core','z'}, dimensions={0} | all-to-all | bytes 458752 | tf_op jit(solution)/shard_map/all_to_all | solution.py:468
  111.1 0.8 collective-permute-start.6
  112.0 1.6 %shard_map.127 = bf16[32,8,128]{2,1,0:T(8,128)(2,1)} custom-call(bf16[896,128]{1,0:T(8,128)(2,1)S(1)} %bitcast.21, s32[8,32]{1,0:T(8,128)S(1)} %get-tuple-element.125.mask, f32[1,128]{1,0:T(1,128)S(1)} %get-tuple-element.126.gain, bf16[128,128]{1,0:T(8,128)(2,1)S(1)} %get-tuple-element.85.w_gate, bf16[256,128]{1,0:T(8,128)(2,1)S(1)} %get-tuple-element.127.d_gate, ...), custom_call_target="tpu_custom_call" | custom-call | tf_op jit(solution)/shard_map/pallas_call | solution.py:449
  113.6 0.0 collective-permute-done.6.recv_near
  113.6 1.0 shard_map.128
  (7 shorter events, 0.1 us)
Async XLA Ops:
  20.6 16.8 %all-to-all-start.1 = ((bf16[16,128,128]{2,1,0:T(8,128)(2,1)}), bf16[16,128,128]{2,1,0:T(8,128)(2,1)S(1)}, u32[]{:S(2)}, u32[]{:S(2)}) async-start(bf16[16,128,128]{2,1,0:T(8,128)(2,1)} %bitcast.5), calls=%async_computation.1 | async-start | bytes 1048576 | tf_op jit(solution)/shard_map/all_to_all | solution.py:468
  27.4 7.2 %collective-permute-start = (bf16[8,4096]{1,0:T(8,128)(2,1)S(1)}, bf16[8,4096]{1,0:T(8,128)(2,1)S(1)}, u32[]{:S(2)}, u32[]{:S(2)}) collective-permute-start(bf16[8,4096]{1,0:T(8,128)(2,1)S(1)} %get-tuple-element.100), channel_id=1, source_target_pairs={{0,16},{4,20},{8,24},{12,28},{16,0},{20,4},{24,8},{28,12},{1,17},{... | collective-permute-start | bytes 196616 | tf_op jit(solution)/shard_map/ppermute | solution.py:472
  29.7 7.7 %collective-permute-start.1 = (bf16[128,256]{1,0:T(8,128)(2,1)S(1)}, bf16[128,256]{1,0:T(8,128)(2,1)S(1)}, u32[]{:S(2)}, u32[]{:S(2)}) collective-permute-start(bf16[128,256]{1,0:T(8,128)(2,1)S(1)} %get-tuple-element.96.own), channel_id=1, source_target_pairs={{0,2},{2,0},{1,3},{3,1},{4,6},{6,4},{5,7},{7,5},{8,10},{10,8},{9,1... | collective-permute-start | bytes 196616 | tf_op jit(solution)/shard_map/ppermute | solution.py:472
  37.4 16.0 %collective-permute-start.2 = (bf16[16,4096]{1,0:T(8,128)(2,1)S(1)}, bf16[16,4096]{1,0:T(8,128)(2,1)S(1)}, u32[]{:S(2)}, u32[]{:S(2)}) collective-permute-start(bf16[16,4096]{1,0:T(8,128)(2,1)S(1)} %constant_dynamic-update-slice_fusion), channel_id=1, source_target_pairs={{0,8},{4,12},{8,0},{12,4},{16,24},{20,28},{24,16},{28,20},{1,9},{5... | collective-permute-start | bytes 393224 | tf_op jit(solution)/shard_map/ppermute | solution.py:472
  53.5 11.9 %collective-permute-start.3 = (bf16[32,4096]{1,0:T(8,128)(2,1)S(1)}, bf16[32,4096]{1,0:T(8,128)(2,1)S(1)}, u32[]{:S(2)}, u32[]{:S(2)}) collective-permute-start(bf16[32,4096]{1,0:T(8,128)(2,1)S(1)} %constant_dynamic-update-slice_fusion.2), channel_id=1, source_target_pairs={{0,1},{1,0},{2,3},{3,2},{4,5},{5,4},{6,7},{7,6},{8,9},{9,8},{10,11... | collective-permute-start | bytes 786440 | tf_op jit(solution)/shard_map/ppermute | solution.py:472
  65.4 16.6 %collective-permute-start.5 = (bf16[64,4096]{1,0:T(8,128)(2,1)S(1)}, bf16[64,4096]{1,0:T(8,128)(2,1)S(1)}, u32[]{:S(2)}, u32[]{:S(2)}) collective-permute-start(bf16[64,4096]{1,0:T(8,128)(2,1)S(1)} %constant_dynamic-update-slice_fusion.4.wide_0), channel_id=1, source_target_pairs={{0,4},{4,0},{8,12},{12,8},{16,20},{20,16},{24,28},{28,24},{1,5},{5... | collective-permute-start | bytes 1572872 | tf_op jit(solution)/shard_map/ppermute | solution.py:472
  68.5 13.5 %all-to-all-start.4 = ((bf16[16,128,128]{2,1,0:T(8,128)(2,1)}), bf16[16,128,128]{2,1,0:T(8,128)(2,1)S(1)}, u32[]{:S(2)}, u32[]{:S(2)}) async-start(bf16[16,128,128]{2,1,0:T(8,128)(2,1)} %bitcast.11), calls=%async_computation.4 | async-start | bytes 1048576 | tf_op jit(solution)/shard_map/all_to_all | solution.py:468
  72.9 4.2 %collective-permute-start.4 = (bf16[256,128]{1,0:T(8,128)(2,1)S(1)}, bf16[256,128]{1,0:T(8,128)(2,1)S(1)}, u32[]{:S(2)}, u32[]{:S(2)}) collective-permute-start(bf16[256,128]{1,0:T(8,128)(2,1)S(1)} %get-tuple-element.114), channel_id=1, source_target_pairs={{0,2},{2,0},{1,3},{3,1},{4,6},{6,4},{5,7},{7,5},{8,10},{10,8},{9,1... | collective-permute-start | bytes 196616 | tf_op jit(solution)/shard_map/ppermute | solution.py:472
  111.1 2.4 %collective-permute-start.6 = (bf16[896,128]{1,0:T(8,128)(2,1)S(1)}, bf16[896,128]{1,0:T(8,128)(2,1)S(1)}, u32[]{:S(2)}, u32[]{:S(2)}) collective-permute-start(bf16[896,128]{1,0:T(8,128)(2,1)S(1)} %bitcast.20), channel_id=1, source_target_pairs={{0,1},{1,0},{2,3},{3,2},{4,5},{5,4},{6,7},{7,6},{8,9},{9,8},{10,11... | collective-permute-start | bytes 688136 | tf_op jit(solution)/shard_map/ppermute | solution.py:472
